TPU v7x, 256 devices: a whole 4x4x8 slice. The times are simulated.
256 devices in a mesh: byte: 32 (over y, x, core), tensor: 8 (over z).
Axes of the slice: x: 4, y: 4, z: 8, core: 2. Of those that a mesh axis runs over, the one named last changes fastest.
Arguments:
- byte_states: bfloat16 [65536, 1280], P(('byte', 'tensor')), may hold values from -6 to 6
- enc_gain: float32 [1280], replicated, may hold values from 0.1 to 1.9
- patch_lengths: int32 [256, 32], P(('byte', 'tensor')), may hold values from 1 to 16, 256 in all within a row
- patch_route: int32 [256, 32, 1], P(('byte', 'tensor')), may hold values from 0 to 31; in each aligned block of 32 rows (0 to 31, 32 to 63, ..., all dimensions but the last counted through in order) at most 2 rows name the same one
- w_in: bfloat16 [1280, 4096], P(None, 'tensor'), may hold values from -0.15625 to 0.15625
- latent_gain: float32 [4096], replicated, may hold values from 0.1 to 1.9
- w_query: bfloat16 [4096, 4096], P('byte', 'tensor'), may hold values from -1 to 1
- w_key: bfloat16 [4096, 4096], P('byte', 'tensor'), may hold values from -24 to 24
- w_value: bfloat16 [4096, 4096], P('byte', 'tensor'), may hold values from -0.09375 to 0.09375
- w_attn_out: bfloat16 [4096, 4096], P('tensor', 'byte'), may hold values from -0.09375 to 0.09375
- w_out: bfloat16 [4096, 1280], P('tensor'), may hold values from -0.09375 to 0.09375
- w_head: bfloat16 [1280, 256], replicated, may hold values from -0.15625 to 0.15625
Outputs:
- logits: bfloat16 [65536, 256], P(('byte', 'tensor'))
Inputs may be any that keep to these rules, and one draw needn't show every extreme that they name: `patch_lengths`: each device's lengths sum to 256; some patch has exactly 16 bytes. `patch_route`: at most 2 patches of one device name the same latent index, and that many are reached.
All inputs are finite; a program needn't handle non-finite values.
Results may differ from a plain program's by a relative error of at most 0.02.
Values may be sent and summed in bfloat16 or wider, within the bound.
A program may use at most 128 MiB of HBM per device.

v0:
```python
import jax
import jax.numpy as jnp
from jax import lax
from jax.sharding import PartitionSpec as P

DH = 128


EPS = 1e-06


def rms_scale(values, scaling):
    values = values.astype(jnp.float32)
    return values * lax.rsqrt(jnp.mean(values * values, axis=-1, keepdims=True) + EPS) * scaling


def patch_tables(lengths, routing, n_dest, capacity, n_bytes):
    ending = jnp.cumsum(lengths)
    starting = ending - lengths
    places = jnp.arange(n_bytes, dtype=jnp.int32)
    member = ((places[None, :] >= starting[:, None]) & (places[None, :] < ending[:, None])).astype(
        jnp.float32
    )
    onehot = (routing[:, None] == jnp.arange(n_dest, dtype=jnp.int32)[None, :]).astype(jnp.int32)
    earlier = jnp.cumsum(onehot, axis=0) - onehot
    slots = jnp.sum(earlier * onehot, axis=1)
    target = routing * capacity + slots
    select = (target[None, :] == jnp.arange(n_dest * capacity, dtype=jnp.int32)[:, None]).astype(
        jnp.float32
    )
    return (member, select)


def attend(queries, key_rows, value_rows, visible_slots, head_size):
    length = queries.shape[0]
    n_heads = queries.shape[1] // head_size
    query_heads = queries.reshape(length, n_heads, head_size)
    key_heads = key_rows.reshape(length, n_heads, head_size)
    value_heads = value_rows.reshape(length, n_heads, head_size)
    scores = jnp.einsum(
        "qhd,khd->hqk", query_heads, key_heads, preferred_element_type=jnp.float32
    ) * head_size ** (-0.5)
    places = jnp.arange(length, dtype=jnp.int32)
    allowed = (places[None, :] < places[:, None]) & (visible_slots[None, :] > 0) | (
        places[None, :] == places[:, None]
    )
    scores = jnp.where(allowed[None, :, :], scores, -1e30)
    highest = jnp.max(scores, axis=-1, keepdims=True)
    raised = jnp.exp(scores - highest)
    weights = (raised / jnp.sum(raised, axis=-1, keepdims=True)).astype(jnp.bfloat16)
    mixed = jnp.einsum("hqk,khd->qhd", weights, value_heads, preferred_element_type=jnp.float32)
    return mixed.astype(jnp.bfloat16).reshape(length, n_heads * head_size)


def body(
    byte_states,
    enc_gain,
    patch_lengths,
    patch_route,
    w_in,
    latent_gain,
    w_query,
    w_key,
    w_value,
    w_attn_out,
    w_out,
    w_head,
):
    byte_count = lax.axis_size("byte")
    byte_rows, byte_width = byte_states.shape
    lengths = patch_lengths[0]
    routing = patch_route[0, :, 0]
    patch_count = lengths.shape[0]
    capacity = max(2, 2 * patch_count // byte_count)
    member, select = patch_tables(lengths, routing, byte_count, capacity, byte_rows)
    normed_bytes = rms_scale(byte_states, enc_gain)
    summed = jnp.dot(
        member, normed_bytes, precision=lax.Precision.HIGHEST, preferred_element_type=jnp.float32
    )
    pooled = (summed / lengths[:, None].astype(jnp.float32)).astype(jnp.bfloat16)
    sending = jnp.dot(
        select.astype(jnp.bfloat16), pooled, preferred_element_type=jnp.float32
    ).astype(jnp.bfloat16)
    used_slots = jnp.sum(select, axis=1).astype(jnp.int32)
    arrived, arrived_used = (
        lax.all_to_all(
            sending.reshape(byte_count, capacity, byte_width),
            "byte",
            split_axis=0,
            concat_axis=0,
            tiled=True,
        ),
        lax.all_to_all(
            used_slots.reshape(byte_count, capacity),
            "byte",
            split_axis=0,
            concat_axis=0,
            tiled=True,
        ),
    )
    own_rows = byte_count * capacity
    local_slots = arrived.reshape(own_rows, byte_width)
    local_used = arrived_used.reshape(own_rows)
    context, context_used = (
        lax.all_gather(local_slots, "tensor", axis=0, tiled=True),
        lax.all_gather(local_used, "tensor", axis=0, tiled=True),
    )
    latent_part = jnp.dot(context, w_in, preferred_element_type=jnp.float32).astype(jnp.bfloat16)
    latent = lax.all_gather(latent_part, "tensor", axis=1, tiled=True)
    latent_normed = rms_scale(latent, latent_gain).astype(jnp.bfloat16)
    inputs = latent_normed
    first = jnp.dot(
        inputs,
        lax.all_gather(w_query, "byte", axis=0, tiled=True),
        preferred_element_type=jnp.float32,
    )
    second = jnp.dot(
        inputs,
        lax.all_gather(w_key, "byte", axis=0, tiled=True),
        preferred_element_type=jnp.float32,
    )
    third = jnp.dot(
        inputs,
        lax.all_gather(w_value, "byte", axis=0, tiled=True),
        preferred_element_type=jnp.float32,
    )
    attended = attend(
        first.astype(jnp.bfloat16),
        second.astype(jnp.bfloat16),
        third.astype(jnp.bfloat16),
        context_used,
        DH,
    )
    partial_value = jnp.dot(
        attended,
        lax.all_gather(w_attn_out, "byte", axis=1, tiled=True),
        preferred_element_type=jnp.float32,
    )
    tensor_place = lax.axis_index("tensor")
    summed_rows = lax.psum_scatter(
        partial_value.astype(jnp.bfloat16), "tensor", scatter_dimension=0, tiled=True
    ).astype(jnp.float32)
    residual = lax.dynamic_slice_in_dim(latent, tensor_place * own_rows, own_rows, 0)
    updated = (residual.astype(jnp.float32) + summed_rows).astype(jnp.bfloat16)
    inputs = updated
    outgoing = jnp.dot(
        inputs,
        lax.all_gather(w_out, "tensor", axis=0, tiled=True),
        preferred_element_type=jnp.float32,
    )
    returned = lax.all_to_all(
        outgoing.astype(jnp.bfloat16).reshape(byte_count, capacity, byte_width),
        "byte",
        split_axis=0,
        concat_axis=0,
        tiled=True,
    )
    patch_values = jnp.dot(
        select.T.astype(jnp.bfloat16),
        returned.reshape(own_rows, byte_width),
        preferred_element_type=jnp.float32,
    )
    spread = jnp.dot(
        member.T, patch_values, precision=lax.Precision.HIGHEST, preferred_element_type=jnp.float32
    )
    decoded = (byte_states.astype(jnp.float32) + spread).astype(jnp.bfloat16)
    return jnp.dot(decoded, w_head, preferred_element_type=jnp.float32).astype(jnp.bfloat16)


def solution(mesh):
    return jax.shard_map(
        body,
        mesh=mesh,
        in_specs=(
            P(("byte", "tensor"), None),
            P(),
            P(("byte", "tensor"), None),
            P(("byte", "tensor"), None, None),
            P(None, "tensor"),
            P(),
            P("byte", "tensor"),
            P("byte", "tensor"),
            P("byte", "tensor"),
            P("tensor", "byte"),
            P("tensor", None),
            P(),
        ),
        out_specs=P(("byte", "tensor"), None),
        check_vma=False,
    )
```

profile of v0, /device:TPU:1, one launch (start us, length us, event | category | flops | bytes accessed | tf_op | source)
XLA Modules:
  0.0 548.2 jit_solution(2065042329873515659)
XLA Ops:
  6.5 0.8 bitcast_convert_fusion
  7.3 0.7 copy.26
  8.1 0.1 reduce
  8.2 0.7 bitcast_subtract_fusion
  8.9 1.3 fusion.11
  10.2 0.7 fusion.25
  11.0 0.8 select_reduce_fusion
  11.8 0.7 multiply_add_fusion
  12.5 1.9 fusion.6
  14.3 0.3 convolution_convert_fusion.2
  14.7 16.3 %all_to_all.16 = bf16[32,2,1280]{2,1,0:T(2,128)(2,1)S(1)} all-to-all(bf16[32,2,1280]{2,1,0:T(2,128)(2,1)S(1)} %reshape.151), channel_id=1, replica_groups=mesh['byte'=32,'tensor'=8] {'byte'}, dimensions={0} | all-to-all | bytes 327680 | tf_op jit(solution)/shard_map/all_to_all | solution.py:86
  31.0 0.7 reshape.152
  31.8 34.3 %all-gather.8.cloned.1.call-done = bf16[512,1280]{1,0:T(8,128)(2,1)} async-done(((bf16[64,1280]{1,0:T(8,128)(2,1)}), bf16[512,1280]{1,0:T(8,128)(2,1)}) %all-gather.8.cloned.1.call-update) | async-done | bytes 1310736 | tf_op jit(solution)/shard_map/all_gather | solution.py:105
  66.2 3.0 convolution_convert_fusion.6
  69.3 0.7 all-gather.16.cloned.1.call-update
  70.0 0.5 all-gather.14.cloned.1.call-update
  70.6 0.5 all-gather.12.cloned.1.call-update
  71.1 0.5 all-gather.18.cloned.1.call-update
  71.8 0.7 convert_element_type.111
  72.5 11.7 %all-to-all-start.1 = ((s32[32,1,2]{2,1,0:T(1,128)}), s32[32,1,2]{2,1,0:T(1,128)S(1)}, u32[]{:S(2)}, u32[]{:S(2)}) async-start(s32[32,1,2]{2,1,0:T(1,128)} %bitcast.4), calls=%async_computation.1 | async-start | bytes 32768 | tf_op jit(solution)/shard_map/all_to_all | solution.py:93
  84.3 0.6 dynamic-slice
  85.5 5.5 %all-to-all-done.1 = s32[32,1,2]{2,1,0:T(1,128)S(1)} async-done(((s32[32,1,2]{2,1,0:T(1,128)}), s32[32,1,2]{2,1,0:T(1,128)S(1)}, u32[]{:S(2)}, u32[]{:S(2)}) %all-to-all-start.1) | async-done | bytes 288 | tf_op jit(solution)/shard_map/all_to_all | solution.py:93
  91.1 0.5 broadcast.66
  91.6 0.7 reduce.4
  92.3 0.1 reshape.160
  92.4 0.2 dynamic-update-slice
  92.6 9.6 %all-reduce = s32[512]{0:T(512)S(1)} all-reduce(s32[512]{0:T(512)S(1)} %dynamic-update-slice), channel_id=1, replica_groups=mesh['byte'=32,'tensor'=8] {'tensor'}, use_global_device_ids=true, to_apply=%add | all-reduce | flops 512 | bytes 4096
  102.3 0.2 fusion.16
  102.4 24.6 %all-gather.10.cloned.1.call-done = bf16[512,4096]{1,0:T(8,128)(2,1)} async-done(((bf16[512,512]{1,0:T(8,128)(2,1)}), bf16[512,4096]{1,0:T(8,128)(2,1)}) %all-gather.10.cloned.1.call-update) | async-done | bytes 4194320 | tf_op jit(solution)/shard_map/all_gather | solution.py:109
  127.0 3.1 fusion.1
  130.1 49.8 %all-gather.16.cloned.1.call-done = bf16[4096,512]{1,0:T(8,128)(2,1)} async-done(((bf16[128,512]{1,0:T(8,128)(2,1)}), bf16[4096,512]{1,0:T(8,128)(2,1)}) %all-gather.16.cloned.1.call-update) | async-done | bytes 4194320 | tf_op jit(solution)/shard_map/all_gather | solution.py:119
  179.9 5.9 %convolution_convert_fusion.3 = bf16[512,512]{0,1:T(8,128)(2,1)S(1)} fusion(bf16[4096,512]{1,0:T(8,128)(2,1)} %all-gather.16.cloned.1.call-done, bf16[512,4096]{1,0:T(8,128)(2,1)} %all-gather.10.cloned.1.call-done, f32[4096]{0:T(1024)S(1)} %copy-done.3, f32[512]{0:T(512)S(1)} %add_rsqrt_fusion), kind=kOutput, calls=%fused_computation.25 | convolution fusion | flops 2156134400 | bytes 8931328 | tf_op jit(solution)/shard_map/dot_general | solution.py:117
  185.9 47.0 %all-gather.14.cloned.1.call-done = bf16[4096,512]{1,0:T(8,128)(2,1)} async-done(((bf16[128,512]{1,0:T(8,128)(2,1)}), bf16[4096,512]{1,0:T(8,128)(2,1)}) %all-gather.14.cloned.1.call-update) | async-done | bytes 4194320 | tf_op jit(solution)/shard_map/all_gather | solution.py:114
  232.9 5.9 %convolution_convert_fusion.4 = bf16[512,512]{0,1:T(8,128)(2,1)S(1)} fusion(bf16[4096,512]{1,0:T(8,128)(2,1)} %all-gather.14.cloned.1.call-done, bf16[512,4096]{1,0:T(8,128)(2,1)} %all-gather.10.cloned.1.call-done, f32[4096]{0:T(1024)S(1)} %copy-done.3, f32[512]{0:T(512)S(1)} %add_rsqrt_fusion), kind=kOutput, calls=%fused_computation.26 | convolution fusion | flops 2156134400 | bytes 8931328 | tf_op jit(solution)/shard_map/dot_general | solution.py:112
  238.8 3.7 fusion.39
  242.5 43.4 %all-gather.12.cloned.1.call-done = bf16[4096,512]{1,0:T(8,128)(2,1)} async-done(((bf16[128,512]{1,0:T(8,128)(2,1)}), bf16[4096,512]{1,0:T(8,128)(2,1)}) %all-gather.12.cloned.1.call-update) | async-done | bytes 4194320 | tf_op jit(solution)/shard_map/all_gather | solution.py:124
  285.8 6.1 %convolution_convert_fusion.5 = bf16[512,512]{0,1:T(8,128)(2,1)S(1)} fusion(bf16[4096,512]{1,0:T(8,128)(2,1)} %all-gather.12.cloned.1.call-done, bf16[512,4096]{1,0:T(8,128)(2,1)} %all-gather.10.cloned.1.call-done, f32[4096]{0:T(1024)S(1)} %copy-done.3, f32[512]{0:T(512)S(1)} %add_rsqrt_fusion), kind=kOutput, calls=%fused_computation.27 | convolution fusion | flops 2156134400 | bytes 8931328 | tf_op jit(solution)/shard_map/dot_general | solution.py:122
  291.9 0.5 fusion.14
  292.4 49.5 %all-gather.18.cloned.1.call-done = bf16[512,4096]{1,0:T(8,128)(2,1)} async-done(((bf16[512,128]{1,0:T(8,128)(2,1)}), bf16[512,4096]{1,0:T(8,128)(2,1)}) %all-gather.18.cloned.1.call-update) | async-done | bytes 4194320 | tf_op jit(solution)/shard_map/all_gather | solution.py:136
  341.9 6.8 %convolution_convert_fusion = bf16[512,4096]{1,0:T(8,128)(2,1)} fusion(bf16[512,512]{0,1:T(8,128)(2,1)S(1)} %bitcast.32, bf16[512,4096]{1,0:T(8,128)(2,1)} %all-gather.18.cloned.1.call-done), kind=kOutput, calls=%fused_computation.6 | convolution fusion | flops 2149580800 | bytes 8912896 | tf_op jit(solution)/shard_map/dot_general | solution.py:134
  348.8 0.7 all-gather.20.cloned.1.call-update
  349.5 53.9 %reduce-scatter.2.cloned.1.call-done = bf16[64,4096]{1,0:T(8,128)(2,1)} async-done(((bf16[512,4096]{1,0:T(8,128)(2,1)}), bf16[64,4096]{1,0:T(8,128)(2,1)}) %reduce-scatter.2.cloned.1.call-update) | async-done | bytes 524304 | tf_op jit(solution)/shard_map/reduce_scatter | solution.py:140
  403.4 114.2 %all-gather.20.cloned.1.call-done = bf16[4096,1280]{1,0:T(8,128)(2,1)} async-done(((bf16[512,1280]{1,0:T(8,128)(2,1)}), bf16[4096,1280]{1,0:T(8,128)(2,1)}) %all-gather.20.cloned.1.call-update) | async-done | bytes 10485776 | tf_op jit(solution)/shard_map/all_gather | solution.py:148
  517.6 6.2 %convolution_convert_fusion.1 = bf16[64,1280]{1,0:T(8,128)(2,1)S(1)} fusion(bf16[4096,1280]{1,0:T(8,128)(2,1)} %all-gather.20.cloned.1.call-done, bf16[64,4096]{1,0:T(8,128)(2,1)} %reduce-scatter.2.cloned.1.call-done, bf16[512,4096]{1,0:T(8,128)(2,1)} %all-gather.10.cloned.1.call-done, s32[]{:T(128)S(6)} %select_n.7), kind=kOutput, calls=%fused_computation.13 | convolution fusion | flops 672219136 | bytes 11698180 | tf_op jit(solution)/shard_map/dot_general | solution.py:146
  523.9 15.3 %all_to_all.17 = bf16[32,2,1280]{2,1,0:T(2,128)(2,1)S(1)} all-to-all(bf16[32,2,1280]{2,1,0:T(2,128)(2,1)S(1)} %reshape.158), channel_id=1, replica_groups=mesh['byte'=32,'tensor'=8] {'byte'}, dimensions={0} | all-to-all | bytes 327680 | tf_op jit(solution)/shard_map/all_to_all | solution.py:151
  539.3 0.2 fusion.30
  539.5 0.8 fusion.5
  540.3 1.0 convolution_convert_fusion.7
  (34 shorter events, 0.8 us)
Async XLA Ops:
  6.5 59.6 %copy-start = (bf16[1280,512]{1,0:T(8,128)(2,1)S(1)}, bf16[1280,512]{1,0:T(8,128)(2,1)}, u32[]{:S(2)}) copy-start(bf16[1280,512]{1,0:T(8,128)(2,1)} %param.16) | copy-start | bytes 3932164
  6.5 59.6 %all-gather.8.cloned.1.call-start = ((), (), s32[]{:S(2)}) async-start(), calls=%async_computation.4 | async-start | bytes 1474560 | tf_op jit(solution)/shard_map/all_gather | solution.py:105
  31.0 53.2 %copy-start.4 = (u32[256]{0:T(256)S(1)}, u32[256]{0:T(256)}, u32[]{:S(2)}) copy-start(u32[256]{0:T(256)} %constant.41) | copy-start | bytes 3076
  31.8 95.3 %all-gather.10.cloned.1.call-start = ((), (), s32[]{:S(2)}) async-start(), calls=%async_computation.5 | async-start | bytes 4718592 | tf_op jit(solution)/shard_map/all_gather | solution.py:109
  69.2 110.7 %copy-start.3 = (f32[4096]{0:T(1024)S(1)}, f32[4096]{0:T(1024)}, u32[]{:S(2)}) copy-start(f32[4096]{0:T(1024)} %param.17) | copy-start | bytes 49156
  69.2 110.7 %all-gather.16.cloned.1.call-start = ((), (), s32[]{:S(2)}) async-start(), calls=%async_computation.8 | async-start | bytes 4325376 | tf_op jit(solution)/shard_map/all_gather | solution.py:119
  69.9 162.9 %all-gather.14.cloned.1.call-start = ((), (), s32[]{:S(2)}) async-start(), calls=%async_computation.7 | async-start | bytes 4325376 | tf_op jit(solution)/shard_map/all_gather | solution.py:114
  70.5 215.3 %all-gather.12.cloned.1.call-start = ((), (), s32[]{:S(2)}) async-start(), calls=%async_computation.6 | async-start | bytes 4325376 | tf_op jit(solution)/shard_map/all_gather | solution.py:124
  71.1 270.8 %all-gather.18.cloned.1.call-start = ((), (), s32[]{:S(2)}) async-start(), calls=%async_computation.9 | async-start | bytes 4325376 | tf_op jit(solution)/shard_map/all_gather | solution.py:136
  72.5 18.6 %all-to-all-start.1 = ((s32[32,1,2]{2,1,0:T(1,128)}), s32[32,1,2]{2,1,0:T(1,128)S(1)}, u32[]{:S(2)}, u32[]{:S(2)}) async-start(s32[32,1,2]{2,1,0:T(1,128)} %bitcast.4), calls=%async_computation.1 | async-start | bytes 32768 | tf_op jit(solution)/shard_map/all_to_all | solution.py:93
  84.2 319.2 %reduce-scatter.2.cloned.1.call-start = ((), (), s32[]{:S(2)}) async-start(), calls=%async_computation.10 | async-start | bytes 4718592 | tf_op jit(solution)/shard_map/reduce_scatter | solution.py:140
  285.8 6.1 %copy-start.5 = (f32[4,512,512]{1,2,0:T(8,128)S(1)}, f32[4,512,512]{1,2,0:T(8,128)}, u32[]{:S(2)}) copy-start(f32[4,512,512]{1,2,0:T(8,128)} %get-tuple-element.6) | copy-start | bytes 12582916
  348.7 168.9 %all-gather.20.cloned.1.call-start = ((), (), s32[]{:S(2)}) async-start(), calls=%async_computation.11 | async-start | bytes 11796480 | tf_op jit(solution)/shard_map/all_gather | solution.py:148
  349.5 190.0 %copy-start.1 = (bf16[256,1280]{1,0:T(8,128)(2,1)S(1)}, bf16[256,1280]{1,0:T(8,128)(2,1)}, u32[]{:S(2)}) copy-start(bf16[256,1280]{1,0:T(8,128)(2,1)} %param.12) | copy-start | bytes 1966084
  349.5 190.8 %copy-start.2 = (bf16[1280,256]{1,0:T(8,128)(2,1)S(1)}, bf16[1280,256]{1,0:T(8,128)(2,1)}, u32[]{:S(2)}) copy-start(bf16[1280,256]{1,0:T(8,128)(2,1)} %param.23) | copy-start | bytes 1966084
Sparse Core Ops, SparseCore 0:
  31.9 34.2 all-gather.7
  69.3 57.6 all-gather.9
  129.6 50.2 all-gather.15
  182.3 50.5 all-gather.13
  235.3 50.5 all-gather.11
  288.2 53.6 all-gather.17
  348.8 54.5 reduce-scatter.1
  405.2 112.3 all-gather.19
where the time goes:
time: 549 us; the launch traced here: 548 us
  waiting for transfers between devices  425 us (77%)
  matrix products  42.2 us (8%)
  blocking collectives  41.3 us (8%)
  between operations  14.3 us (3%)
  starting transfers between devices  12 us (2%)
  other arithmetic  9.23 us (2%)
    all_gather x1, waiting for transfers between devices, body(): lax.all_gather(w_out, 'tensor', axis=0, tiled=True)  114 us
    reduce_scatter x1, waiting for transfers between devices, body(): lax.psum_scatter(partial_value.astype(jnp.bfloat16), 'tensor', scatter_di...  53.9 us
    all_gather x1, waiting for transfers between devices, body(): lax.all_gather(w_key, 'byte', axis=0, tiled=True)  49.8 us
    all_gather x1, waiting for transfers between devices, body(): lax.all_gather(w_attn_out, 'byte', axis=1, tiled=True)  49.5 us
    all_gather x1, waiting for transfers between devices, body(): lax.all_gather(w_query, 'byte', axis=0, tiled=True)  47 us
    all_gather x1, waiting for transfers between devices, body(): lax.all_gather(w_value, 'byte', axis=0, tiled=True)  43.4 us
    all_gather x1, waiting for transfers between devices, body(): lax.all_gather(local_slots, 'tensor', axis=0, tiled=True)  34.3 us
    all_gather x1, waiting for transfers between devices, body(): latent = lax.all_gather(latent_part, 'tensor', axis=1, tiled=True)  24.6 us
  transfers between devices with their start and end apart: 9, of which 9 were waited for; matrix products, arithmetic and copies ran while one was open for 5% of the time, Pallas kernels for 0%

commit v1 on v0

v1 whole, which is shorter than its diff:
```python
import jax
import jax.numpy as jnp
from jax import lax
from jax.sharding import PartitionSpec as P

DH = 128


EPS = 1e-06


def rms_scale(values, scaling):
    values = values.astype(jnp.float32)
    return values * lax.rsqrt(jnp.mean(values * values, axis=-1, keepdims=True) + EPS) * scaling


def patch_tables(lengths, routing, n_dest, capacity, n_bytes):
    ending = jnp.cumsum(lengths)
    starting = ending - lengths
    places = jnp.arange(n_bytes, dtype=jnp.int32)
    member = ((places[None, :] >= starting[:, None]) & (places[None, :] < ending[:, None])).astype(
        jnp.float32
    )
    onehot = (routing[:, None] == jnp.arange(n_dest, dtype=jnp.int32)[None, :]).astype(jnp.int32)
    earlier = jnp.cumsum(onehot, axis=0) - onehot
    slots = jnp.sum(earlier * onehot, axis=1)
    target = routing * capacity + slots
    select = (target[None, :] == jnp.arange(n_dest * capacity, dtype=jnp.int32)[:, None]).astype(
        jnp.float32
    )
    return (member, select)


def attend(queries, key_rows, value_rows, visible_slots, head_size):
    length = queries.shape[0]
    n_heads = queries.shape[1] // head_size
    query_heads = queries.reshape(length, n_heads, head_size)
    key_heads = key_rows.reshape(length, n_heads, head_size)
    value_heads = value_rows.reshape(length, n_heads, head_size)
    scores = jnp.einsum(
        "qhd,khd->hqk", query_heads, key_heads, preferred_element_type=jnp.float32
    ) * head_size ** (-0.5)
    places = jnp.arange(length, dtype=jnp.int32)
    allowed = (places[None, :] < places[:, None]) & (visible_slots[None, :] > 0) | (
        places[None, :] == places[:, None]
    )
    scores = jnp.where(allowed[None, :, :], scores, -1e30)
    highest = jnp.max(scores, axis=-1, keepdims=True)
    raised = jnp.exp(scores - highest)
    weights = (raised / jnp.sum(raised, axis=-1, keepdims=True)).astype(jnp.bfloat16)
    mixed = jnp.einsum("hqk,khd->qhd", weights, value_heads, preferred_element_type=jnp.float32)
    return mixed.astype(jnp.bfloat16).reshape(length, n_heads * head_size)


def dot(a, b):
    return jnp.dot(a, b, preferred_element_type=jnp.float32)


def body(
    byte_states,
    enc_gain,
    patch_lengths,
    patch_route,
    w_in,
    latent_gain,
    w_query,
    w_key,
    w_value,
    w_attn_out,
    w_out,
    w_head,
):
    byte_count = lax.axis_size("byte")
    byte_place = lax.axis_index("byte")
    tensor_place = lax.axis_index("tensor")
    byte_rows, byte_width = byte_states.shape
    depth = w_query.shape[0]
    columns = w_in.shape[1]
    per = columns // depth

    holder = tensor_place == byte_place // per
    offset = (byte_place % per) * depth
    sub_in = lax.dynamic_slice_in_dim(w_in, offset, depth, 1)
    sub_out = lax.dynamic_slice_in_dim(w_out, offset, depth, 0)
    both = jnp.concatenate([sub_in.T, sub_out], axis=0)
    both = lax.psum(jnp.where(holder, both, jnp.zeros_like(both)), "tensor")
    gain = lax.dynamic_slice_in_dim(latent_gain, byte_place * depth, depth, 0)
    sub_in = (both[:depth].astype(jnp.float32) * gain[:, None]).astype(jnp.bfloat16)
    sub_out = both[depth:]
    parts = [
        lax.dot_general(
            left, weight, (((0,), (0,)), ((), ())), preferred_element_type=jnp.float32
        ).astype(jnp.bfloat16)
        for left, weight in (
            (sub_in, w_query),
            (sub_in, w_key),
            (sub_in, w_value),
            (sub_out, w_attn_out.T),
        )
    ]
    partial = jnp.concatenate(parts, axis=0)
    shares = lax.psum_scatter(partial, "byte", scatter_dimension=0, tiled=True)
    fused = lax.all_gather(shares, "byte", axis=0, tiled=True)
    m_query, m_key, m_value, m_out = jnp.split(fused, 4, axis=0)

    lengths = patch_lengths[0]
    routing = patch_route[0, :, 0]
    patch_count = lengths.shape[0]
    capacity = max(2, 2 * patch_count // byte_count)
    member, select = patch_tables(lengths, routing, byte_count, capacity, byte_rows)
    normed_bytes = rms_scale(byte_states, enc_gain)
    summed = jnp.dot(
        member, normed_bytes, precision=lax.Precision.HIGHEST, preferred_element_type=jnp.float32
    )
    pooled = (summed / lengths[:, None].astype(jnp.float32)).astype(jnp.bfloat16)
    sending = dot(select.astype(jnp.bfloat16), pooled).astype(jnp.bfloat16)
    used_slots = jnp.sum(select, axis=1).astype(jnp.bfloat16)
    sending = jnp.concatenate(
        [sending, jnp.broadcast_to(used_slots[:, None], (sending.shape[0], 128))], axis=1
    )
    width = byte_width + 128
    arrived = lax.all_to_all(
        sending.reshape(byte_count, capacity, width),
        "byte",
        split_axis=0,
        concat_axis=0,
        tiled=True,
    )
    own_rows = byte_count * capacity
    context = lax.all_gather(arrived.reshape(own_rows, width), "tensor", axis=0, tiled=True)
    context_used = context[:, byte_width]
    context = context[:, :byte_width]
    latent_part = dot(context, w_in).astype(jnp.bfloat16)
    squares = jnp.sum(jnp.square(latent_part.astype(jnp.float32)), axis=-1)
    squares = lax.psum(squares, "tensor")
    scale = lax.rsqrt(squares / latent_gain.shape[0] + EPS)[:, None]
    attended = attend(
        (dot(context, m_query) * scale).astype(jnp.bfloat16),
        (dot(context, m_key) * scale).astype(jnp.bfloat16),
        (dot(context, m_value) * scale).astype(jnp.bfloat16),
        context_used,
        DH,
    )
    partial_value = dot(latent_part, w_out) + lax.dot_general(
        attended, m_out, (((1,), (1,)), ((), ())), preferred_element_type=jnp.float32
    )
    outgoing = lax.psum_scatter(
        partial_value.astype(jnp.bfloat16), "tensor", scatter_dimension=0, tiled=True
    )
    returned = lax.all_to_all(
        outgoing.reshape(byte_count, capacity, byte_width),
        "byte",
        split_axis=0,
        concat_axis=0,
        tiled=True,
    )
    patch_values = dot(select.T.astype(jnp.bfloat16), returned.reshape(own_rows, byte_width))
    spread = jnp.dot(
        member.T, patch_values, precision=lax.Precision.HIGHEST, preferred_element_type=jnp.float32
    )
    decoded = (byte_states.astype(jnp.float32) + spread).astype(jnp.bfloat16)
    return dot(decoded, w_head).astype(jnp.bfloat16)


def solution(mesh):
    return jax.shard_map(
        body,
        mesh=mesh,
        in_specs=(
            P(("byte", "tensor"), None),
            P(),
            P(("byte", "tensor"), None),
            P(("byte", "tensor"), None, None),
            P(None, "tensor"),
            P(),
            P("byte", "tensor"),
            P("byte", "tensor"),
            P("byte", "tensor"),
            P("tensor", "byte"),
            P("tensor", None),
            P(),
        ),
        out_specs=P(("byte", "tensor"), None),
        check_vma=False,
    )
```

time: 549 us -> 377 us (0.69)
  waiting for transfers between devices: 425 us -> 256 us
  matrix products: 42.2 us -> 26.6 us
  other arithmetic: 9.23 us -> 22.4 us
  starting transfers between devices: 12 us -> 0.17 us
  blocking collectives: 41.3 us -> 52.1 us
    all_gather x7 -> x2, waiting for transfers between devices: 363 us -> 77.9 us  [the longest x1 39.4 us: body(): fused = lax.all_gather(shares, 'byte', axis=0, tiled=True)]
    psum x0 -> x1, waiting for transfers between devices: none -> 73.5 us  [body(): both = lax.psum(jnp.where(holder, both, jnp.zeros_like(both)), 'tensor')]
    reduce_scatter x0 -> x1, waiting for transfers between devices: none -> 69.9 us  [body(): shares = lax.psum_scatter(partial, 'byte', scatter_dimension=0, tiled=True)]
    reduce_scatter x1, waiting for transfers between devices: 53.9 us -> 34.4 us  [body(): lax.psum_scatter(partial_value.astype(jnp.bfloat16), 'tensor', scatter_di...]
    concatenate x0 -> x2, other arithmetic: none -> 19.4 us  [the longest x1 19.4 us: body(): partial = jnp.concatenate(parts, axis=0)]
    dot_general x9 -> x13, matrix products: 35.4 us -> 20.8 us  [the longest x8 14.1 us: dot(): return jnp.dot(a, b, preferred_element_type=jnp.float32)]
    psum x0 -> x1, blocking collectives: none -> 12.7 us  [body(): squares = lax.psum(squares, 'tensor')]
    all_to_all x1 -> x0, starting transfers between devices: 11.7 us -> none  [body(): lax.all_to_all(used_slots.reshape(byte_count, capacity), 'byte', split_ax...]
  transfers between devices with their start and end apart: 9 -> 5, of which waited for: 9 -> 5; matrix products, arithmetic and copies ran while one was open for 5% -> 3% of each run, Pallas kernels for 0% -> 0%
where the time goes in v1:
time: 377 us
  waiting for transfers between devices  256 us (68%)
  blocking collectives  52.1 us (14%)
  matrix products  26.6 us (7%)
  other arithmetic  22.4 us (6%)
  between operations  13.4 us (4%)
  local copies, waits for them, and re-layouts  6.3 us (2%)
    psum x1, waiting for transfers between devices, body(): both = lax.psum(jnp.where(holder, both, jnp.zeros_like(both)), 'tensor')  73.5 us
    reduce_scatter x1, waiting for transfers between devices, body(): shares = lax.psum_scatter(partial, 'byte', scatter_dimension=0, tiled=True)  69.9 us
    all_gather x1, waiting for transfers between devices, body(): fused = lax.all_gather(shares, 'byte', axis=0, tiled=True)  39.4 us
    all_gather x1, waiting for transfers between devices, body(): lax.all_gather(arrived.reshape(own_rows, width), 'tensor', axis=0, tiled=...  38.5 us
    reduce_scatter x1, waiting for transfers between devices, body(): lax.psum_scatter(partial_value.astype(jnp.bfloat16), 'tensor', scatter_di...  34.4 us
    all_to_all x1, blocking collectives, body(): lax.all_to_all(sending.reshape(byte_count, capacity, width), 'byte', spli...  19.8 us
    all_to_all x1, blocking collectives, body(): lax.all_to_all(outgoing.reshape(byte_count, capacity, byte_width), 'byte'...  19.5 us
    concatenate x1, other arithmetic, body(): partial = jnp.concatenate(parts, axis=0)  19.4 us
  transfers between devices with their start and end apart: 5, of which 5 were waited for; matrix products, arithmetic and copies ran while one was open for 3% of the time, Pallas kernels for 0%

profile of v1, /device:TPU:1, one launch (start us, length us, event | category | flops | bytes accessed | tf_op | source)
XLA Modules:
  0.0 376.8 jit_solution(7695552998288727157)
XLA Ops:
  6.5 1.1 constant_dynamic-slice_fusion.1
  7.6 0.2 copy.37
  7.8 0.1 copy-done
  8.0 1.0 maximum_select_fusion
  9.1 0.8 dynamic_slice.11
  9.8 73.5 %all-reduce.2.cloned.1.call-done = bf16[256,1280]{1,0:T(8,128)(2,1)} async-done(((bf16[256,1280]{1,0:T(8,128)(2,1)}), bf16[256,1280]{1,0:T(8,128)(2,1)}) %all-reduce.2.cloned.1.call-update) | async-done | bytes 655376 | tf_op jit(solution)/shard_map/psum | solution.py:86
  83.3 1.6 convolution_convert_fusion.1
  85.0 0.6 convolution_convert_fusion.2
  85.6 0.6 convolution_convert_fusion.3
  86.2 0.5 convolution_convert_fusion
  86.7 19.4 %pad_maximum_fusion = bf16[5120,512]{1,0:T(8,128)(2,1)} fusion(bf16[1280,512]{1,0:T(8,128)(2,1)S(1)} %convolution_convert_fusion, bf16[1280,512]{1,0:T(8,128)(2,1)S(1)} %convolution_convert_fusion.1, bf16[1280,512]{1,0:T(8,128)(2,1)S(1)} %convolution_convert_fusion.2, bf16[1280,512]{1,0:T(8,128)(2,1)S(1)} %convolution_convert_fusion.3), kind=kLoop, calls=%fused_computation.1 | loop fusion | flops 20971520 | bytes 10485760 | tf_op jit(solution)/shard_map/concatenate | solution.py:101
  106.2 0.6 copy-done.11
  106.8 0.1 copy.29
  106.9 0.1 reduce
  107.0 0.1 fusion.40
  107.1 0.1 reduce_window_sum.18
  107.2 0.2 select_reduce_fusion
  107.3 0.1 convert_reduce_fusion
  107.4 0.2 fusion.9
  107.7 0.8 fusion.4
  108.5 0.3 convolution_convert_fusion.4
  108.8 0.1 broadcast_in_dim.12
  108.9 0.1 reshape.135
  109.0 19.8 %all_to_all.10 = bf16[32,2,1408]{2,1,0:T(2,128)(2,1)S(1)} all-to-all(bf16[32,2,1408]{2,1,0:T(2,128)(2,1)S(1)} %reshape.135), channel_id=1, replica_groups=mesh['byte'=32,'tensor'=8] {'byte'}, dimensions={0} | all-to-all | bytes 360448 | tf_op jit(solution)/shard_map/all_to_all | solution.py:122
  128.8 0.7 reshape.136
  129.6 69.9 %reduce-scatter.3.cloned.1.call-done = bf16[160,512]{1,0:T(8,128)(2,1)} async-done(((bf16[5120,512]{1,0:T(8,128)(2,1)}), bf16[160,512]{1,0:T(8,128)(2,1)}) %reduce-scatter.3.cloned.1.call-update) | async-done | bytes 163856 | tf_op jit(solution)/shard_map/reduce_scatter | solution.py:102
  199.6 38.5 %all-gather.3.cloned.1.call-done = bf16[512,1408]{1,0:T(8,128)(2,1)} async-done(((bf16[64,1408]{1,0:T(8,128)(2,1)}), bf16[512,1408]{1,0:T(8,128)(2,1)}) %all-gather.3.cloned.1.call-update) | async-done | bytes 1441808 | tf_op jit(solution)/shard_map/all_gather | solution.py:130
  238.1 2.6 multiply_reduce_fusion
  240.7 12.7 %psum.15 = f32[512]{0:T(512)S(1)} all-reduce(f32[512]{0:T(512)S(1)} %get-tuple-element.5), channel_id=1, replica_groups=mesh['byte'=32,'tensor'=8] {'tensor'}, use_global_device_ids=true, to_apply=%region_8.9 | all-reduce | flops 512 | bytes 4096 | tf_op jit(solution)/shard_map/psum | solution.py:135
  253.5 1.1 compare_reduce_fusion
  254.5 0.2 fusion.27
  254.7 2.3 fusion.51
  257.1 39.4 %all-gather.5.cloned.1.call-done = bf16[5120,512]{1,0:T(8,128)(2,1)} async-done(((bf16[160,512]{1,0:T(8,128)(2,1)}), bf16[5120,512]{1,0:T(8,128)(2,1)}) %all-gather.5.cloned.1.call-update) | async-done | bytes 5242896 | tf_op jit(solution)/shard_map/all_gather | solution.py:103
  296.4 2.7 fusion.22
  299.2 2.2 fusion.19
  301.4 3.7 fusion.50
  305.1 2.7 fusion.16
  307.9 0.2 copy-done.13
  308.1 0.5 fusion.25
  308.6 1.2 copy-done.1
  309.8 3.3 fusion.2
  313.2 34.4 %reduce-scatter.5.cloned.1.call-done = bf16[64,1280]{1,0:T(8,128)(2,1)} async-done(((bf16[512,1280]{1,0:T(8,128)(2,1)}), bf16[64,1280]{1,0:T(8,128)(2,1)}) %reduce-scatter.5.cloned.1.call-update) | async-done | bytes 163856 | tf_op jit(solution)/shard_map/reduce_scatter | solution.py:147
  347.6 1.0 reshape.141
  348.6 19.5 %all_to_all.11 = bf16[32,2,1280]{2,1,0:T(2,128)(2,1)S(1)} all-to-all(bf16[32,2,1280]{2,1,0:T(2,128)(2,1)S(1)} %reshape.141), channel_id=1, replica_groups=mesh['byte'=32,'tensor'=8] {'byte'}, dimensions={0} | all-to-all | bytes 327680 | tf_op jit(solution)/shard_map/all_to_all | solution.py:150
  368.1 0.1 reshape.142
  368.2 0.2 fusion.45
  368.4 0.8 fusion.3
  369.2 1.0 convolution_convert_fusion.6
  (42 shorter events, 0.4 us)
Async XLA Ops:
  6.5 1.4 copy-start
  6.5 76.7 %all-reduce.2.cloned.1.call-start = ((), (), s32[]{:S(2)}) async-start(), calls=%async_computation.5 | async-start | bytes 1310720 | tf_op jit(solution)/shard_map/psum | solution.py:86
  8.0 75.3 %copy-start.6 = (bf16[128,512]{1,0:T(8,128)(2,1)S(1)}, bf16[128,512]{1,0:T(8,128)(2,1)}, u32[]{:S(2)}) copy-start(bf16[128,512]{1,0:T(8,128)(2,1)} %param.20) | copy-start | bytes 393220
  9.0 76.0 %copy-start.7 = (bf16[128,512]{1,0:T(8,128)(2,1)S(1)}, bf16[128,512]{1,0:T(8,128)(2,1)}, u32[]{:S(2)}) copy-start(bf16[128,512]{1,0:T(8,128)(2,1)} %param.19) | copy-start | bytes 393220
  9.0 190.5 %reduce-scatter.3.cloned.1.call-start = ((), (), s32[]{:S(2)}) async-start(), calls=%async_computation.6 | async-start | bytes 5406720 | tf_op jit(solution)/shard_map/reduce_scatter | solution.py:102
  9.8 75.8 %copy-start.8 = (bf16[128,512]{1,0:T(8,128)(2,1)S(1)}, bf16[128,512]{1,0:T(8,128)(2,1)}, u32[]{:S(2)}) copy-start(bf16[128,512]{1,0:T(8,128)(2,1)} %param.18) | copy-start | bytes 393220
  83.3 1.7 copy-start.3
  85.0 1.2 copy-start.5
  106.1 0.7 copy-start.11
  106.1 0.9 copy-start.10
  106.1 1.3 copy-start.2
  106.1 1.6 copy-start.12
  106.1 132.0 %all-gather.3.cloned.1.call-start = ((), (), s32[]{:S(2)}) async-start(), calls=%async_computation.4 | async-start | bytes 1622016 | tf_op jit(solution)/shard_map/all_gather | solution.py:130
  129.5 166.9 %all-gather.5.cloned.1.call-start = ((), (), s32[]{:S(2)}) async-start(), calls=%async_computation.7 | async-start | bytes 5406720 | tf_op jit(solution)/shard_map/all_gather | solution.py:103
  199.5 148.1 %reduce-scatter.5.cloned.1.call-start = ((), (), s32[]{:S(2)}) async-start(), calls=%async_computation.8 | async-start | bytes 1474560 | tf_op jit(solution)/shard_map/reduce_scatter | solution.py:147
  296.4 2.7 copy-start.9
  305.1 3.0 copy-start.13
  308.1 1.7 copy-start.1
  313.2 56.0 %copy-start.4 = (bf16[1280,256]{1,0:T(8,128)(2,1)S(1)}, bf16[1280,256]{1,0:T(8,128)(2,1)}, u32[]{:S(2)}) copy-start(bf16[1280,256]{1,0:T(8,128)(2,1)} %param.23) | copy-start | bytes 1966084
Sparse Core Ops, SparseCore 0:
  9.7 73.5 all-reduce.1
  106.3 93.2 reduce-scatter.2
  201.4 36.6 all-gather.2
  240.8 55.5 all-gather.4
  313.3 34.2 reduce-scatter.4

commit v2 on v1

v2 whole, which is shorter than its diff:
```python
import jax
import jax.numpy as jnp
from jax import lax
from jax.experimental import pallas as pl
from jax.experimental.pallas import tpu as pltpu
from jax.sharding import PartitionSpec as P

MESH = pl.DeviceIdType.MESH
BF16 = jnp.bfloat16
F32 = jnp.float32
DH = 128
EPS = 1e-06
SIDE = 4
NB = 32
NT = 8
E = 1280
D = 4096
CTX = 512
W = 256
PIECES = E // W
STAGES = 2 * PIECES
FLAGS = 128
PACK = 16


def mm(a, b):
    return jnp.dot(a, b, preferred_element_type=F32)


def mm_t(a, b):
    return lax.dot_general(a, b, (((1,), (1,)), ((), ())), preferred_element_type=F32)


def iota(shape, dim):
    return lax.broadcasted_iota(jnp.int32, shape, dim)


def onehot(mask):
    return jnp.where(mask, 1.0, 0.0).astype(BF16)


def tables(lengths, route):
    n = lengths.shape[1]
    down, across = iota((n, n), 0), iota((n, n), 1)
    eye = down == across

    def column(row):
        return jnp.sum(jnp.where(eye, row, 0.0), axis=1, keepdims=True)

    len_row = lengths[...].astype(F32)
    route_row = route[...].astype(F32)
    len_col, route_col = column(len_row), column(route_row)
    end_row = jnp.sum(jnp.where(down <= across, len_col, 0.0), axis=0, keepdims=True)
    end_col = jnp.sum(jnp.where(across <= down, len_row, 0.0), axis=1, keepdims=True)
    same = jnp.where(route_row == route_col, 1.0, 0.0)
    slot_row = jnp.sum(jnp.where(down < across, same, 0.0), axis=0, keepdims=True)
    slot_col = jnp.sum(jnp.where(across < down, same, 0.0), axis=1, keepdims=True)
    return len_row, len_col, route_row, route_col, end_row, end_col, slot_row, slot_col


def kernel(
    states, gain, lengths, route, w_in, lat_gain, w_q, w_k, w_v, w_ao, w_out, w_head, out,
    blk, wsc, wx, wxo, p_q, p_o, r1_q, r1_o, t_q, t_o, r2_q, r2_o, m_q, m_o,
    snd, arr, snd2, arr2, ctx, lat, sqs, acc, qkv, att, lw, zp, zr, packf,
    w_s, w_r, p_s, p_r, loc, x_s, x_r, a_s, a_r, c_s, c_r, q_s, q_r,
    r1_s, r1_r, r2_s, r2_r, g1_s, g1_r, g2_s, g2_r, h_s, h_r, z_s, z_r, b_s, b_r,
):
    b = lax.axis_index("byte")
    t = lax.axis_index("tensor")
    k = b % 2
    chip = b // 2
    x = chip % SIDE
    y = chip // SIDE
    far = (t - chip // 2 + NT) % NT
    up = (b, (t + 1) % NT)
    down = (b, (t + NT - 1) % NT)
    partner = (b + 1 - 2 * k, t)
    sends = []

    def rcopy(src, dst, ssem, rsem, dev):
        return pltpu.make_async_remote_copy(
            src_ref=src, dst_ref=dst, send_sem=ssem, recv_sem=rsem, device_id=dev, device_id_type=MESH
        )

    def send(src, dst, ssem, rsem, dev):
        copy = rcopy(src, dst, ssem, rsem, dev)
        copy.start()
        sends.append(copy)

    def got(dst, ssem, rsem, dev):
        rcopy(dst, dst, ssem, rsem, dev).wait_recv()

    def rows(start, size, step=16):
        return pl.ds(pl.multiple_of(start, step), size)

    bar = pltpu.get_barrier_semaphore()

    @pl.loop(1, NB)
    def _(i):
        pl.semaphore_signal(bar, inc=1, device_id=((b + i) % NB, t), device_id_type=MESH)

    @pl.loop(1, NT)
    def _(i):
        pl.semaphore_signal(bar, inc=1, device_id=(b, (t + i) % NT), device_id_type=MESH)

    g_row = lat_gain[pl.ds(b, 1), :]
    eye = iota((128, 128), 0) == iota((128, 128), 1)
    g_col = jnp.sum(jnp.where(eye, g_row, 0.0), axis=1, keepdims=True)
    half = rows(128 * k, 128, 128)
    mine = rows(W * k, W, W)
    theirs = rows(W * (1 - k), W, W)
    for m, weight in enumerate((w_q, w_k, w_v)):
        wsc[m] = (weight[...].astype(F32) * g_col).astype(BF16)

    pl.semaphore_wait(bar, NB + NT - 2)

    for m in range(3):
        send(wsc.at[m, :, theirs], wx.at[m, half, :], x_s.at[m], x_r.at[m], partner)
    send(w_ao.at[theirs, :], wxo.at[:, half], x_s.at[3], x_r.at[3], partner)

    off = rows(W * (chip % 2), W, W)

    def relay(j):
        piece = blk.at[j, half, :]
        if j < PIECES:
            source = w_in.at[rows(W * j + 128 * k, 128, 128), off]
            whole = w_in.at[pl.ds(W * j, W), off]
        else:
            cols = pl.ds(W * (j - PIECES), W)
            source = w_out.at[rows(W * (chip % 2) + 128 * k, 128, 128), cols]
            whole = w_out.at[off, cols]

        @pl.when(far == 0)
        def _():
            rcopy(source, piece, w_s.at[j, 0], w_r.at[j], up).start()
            rcopy(source, piece, w_s.at[j, 1], w_r.at[j], down).start()
            pltpu.make_async_copy(whole, blk.at[j], loc.at[j]).start()

        @pl.when(far != 0)
        def _():
            got(piece, w_s.at[j, 0], w_r.at[j], up)

            @pl.when(far <= 3)
            def _():
                rcopy(piece, piece, w_s.at[j, 0], w_r.at[j], up).start()

            @pl.when(far >= 6)
            def _():
                rcopy(piece, piece, w_s.at[j, 1], w_r.at[j], down).start()

            rcopy(piece, piece, p_s.at[j], p_r.at[j], partner).start()

    def relay_end(j):
        piece = blk.at[j, half, :]

        @pl.when(far <= 3)
        def _():
            rcopy(piece, piece, w_s.at[j, 0], w_r.at[j], up).wait_send()

        @pl.when((far == 0) | (far >= 6))
        def _():
            rcopy(piece, piece, w_s.at[j, 1], w_r.at[j], down).wait_send()

        @pl.when(far != 0)
        def _():
            rcopy(piece, piece, p_s.at[j], p_r.at[j], partner).wait_send()

    def layout(j):
        if j < PIECES:
            return j, 3 * W // 16, p_q, r1_q, t_q, r2_q, m_q
        return j - PIECES, W // 16, p_o, r1_o, t_o, r2_o, m_o

    def axes(j):
        return (x, y) if j % 2 == 0 else (y, x)

    def peer(j, first, i):
        along_x = (j % 2 == 0) == first
        px = (x + i) % SIDE if along_x else x
        py = y if along_x else (y + i) % SIDE
        return ((py * SIDE + px) * 2 + k, t)

    def product(j):
        other = blk.at[j, rows(128 * (1 - k), 128, 128), :]

        @pl.when(far == 0)
        def _():
            pltpu.make_async_copy(blk.at[j], blk.at[j], loc.at[j]).wait()

        @pl.when(far != 0)
        def _():
            got(other, p_s.at[j], p_r.at[j], partner)

        if j == 0:
            for m in range(3):
                got(wx.at[m, rows(128 * (1 - k), 128, 128), :], x_s.at[m], x_r.at[m], partner)
                wx[m, half, :] = wsc[m, :, mine]
        if j == PIECES:
            got(wxo.at[:, rows(128 * (1 - k), 128, 128)], x_s.at[3], x_r.at[3], partner)
            wxo[:, half] = w_ao[mine, :]
        n, part, p, r1, tt, r2, m_ = layout(j)
        if j < PIECES:
            for m in range(3):
                p[n, W * m : W * (m + 1), :] = mm(blk[j], wx[m]).astype(BF16)
        else:
            p[n] = mm(wxo[...], blk[j]).astype(BF16)
        u, v = axes(j)
        for i in range(1, SIDE):
            to = (u + i) % SIDE
            send(
                p.at[n, rows(4 * part * to, 4 * part), :], r1.at[n, i - 1],
                r1_s.at[j, i - 1], r1_r.at[j, i - 1], peer(j, True, i),
            )

    def first_sum(j):
        n, part, p, r1, tt, r2, m_ = layout(j)
        u, v = axes(j)
        for i in range(1, SIDE):
            got(r1.at[n, i - 1], r1_s.at[j, i - 1], r1_r.at[j, i - 1], peer(j, True, i))
        total = p[n, rows(4 * part * u, 4 * part), :].astype(F32)
        for i in range(SIDE - 1):
            total = total + r1[n, i].astype(F32)
        tt[n] = total.astype(BF16)
        for i in range(1, SIDE):
            to = (v + i) % SIDE
            send(
                tt.at[n, rows(part * to, part), :], r2.at[n, i - 1],
                r2_s.at[j, i - 1], r2_r.at[j, i - 1], peer(j, False, i),
            )

    def second_sum(j):
        n, part, p, r1, tt, r2, m_ = layout(j)
        u, v = axes(j)
        for i in range(1, SIDE):
            got(r2.at[n, i - 1], r2_s.at[j, i - 1], r2_r.at[j, i - 1], peer(j, False, i))
        total = tt[n, rows(part * v, part), :].astype(F32)
        for i in range(SIDE - 1):
            total = total + r2[n, i].astype(F32)
        own = rows(part * (4 * u + v), part)
        m_[n, k, own, :] = total.astype(BF16)
        for i in range(1, SIDE):
            send(
                m_.at[n, k, own, :], m_.at[n, k, own, :],
                g1_s.at[j, i - 1], g1_r.at[j, i - 1], peer(j, False, i),
            )

    def first_gather(j):
        n, part, p, r1, tt, r2, m_ = layout(j)
        u, v = axes(j)
        for i in range(1, SIDE):
            came = rows(part * (4 * u + (v + SIDE - i) % SIDE), part)
            got(m_.at[n, k, came, :], g1_s.at[j, i - 1], g1_r.at[j, i - 1], peer(j, False, i))
        own = rows(4 * part * u, 4 * part)
        for i in range(1, SIDE):
            send(
                m_.at[n, k, own, :], m_.at[n, k, own, :],
                g2_s.at[j, i - 1], g2_r.at[j, i - 1], peer(j, True, i),
            )

    def second_gather(j):
        n, part, p, r1, tt, r2, m_ = layout(j)
        u, v = axes(j)
        for i in range(1, SIDE):
            came = rows(4 * part * ((u + SIDE - i) % SIDE), 4 * part)
            got(m_.at[n, k, came, :], g2_s.at[j, i - 1], g2_r.at[j, i - 1], peer(j, True, i))
        send(m_.at[n, k], m_.at[n, k], h_s.at[j], h_r.at[j], partner)

    def joined(j):
        n, part, p, r1, tt, r2, m_ = layout(j)
        got(m_.at[n, 1 - k], h_s.at[j], h_r.at[j], partner)
        if j < PIECES:
            piece = ctx[:, W * j : W * (j + 1)]
            for m in range(3):
                for side in range(2):
                    cols = slice(W * side, W * (side + 1))
                    term = mm(piece, m_[n, side, W * m : W * (m + 1), :])
                    if j == 0:
                        acc[m, :, cols] = term
                    else:
                        acc[m, :, cols] = acc[m, :, cols] + term

    def pool():
        len_row, len_col, route_row, route_col, end_row, end_col, slot_row, slot_col = tables(
            lengths, route
        )
        values = states[...].astype(F32)
        scale = lax.rsqrt(jnp.mean(values * values, axis=-1, keepdims=True) + EPS)
        normed = values * scale * gain[...]
        high = normed.astype(BF16)
        low = (normed - high.astype(F32)).astype(BF16)
        n = states.shape[0]
        place = iota((lengths.shape[1], n), 1).astype(F32)
        member = onehot((place >= end_col - len_col) & (place < end_col))
        pooled = ((mm(member, high) + mm(member, low)) / len_col).astype(BF16)
        spot = iota((NB * PACK, lengths.shape[1]), 0).astype(F32)
        target = route_row * PACK + slot_row * PIECES
        packed = mm(
            onehot(spot == route_row * PACK + 2 * PIECES + slot_row),
            jnp.ones((lengths.shape[1], W), BF16),
        )
        for j in range(PIECES):
            packed = packed + mm(onehot(spot == target + j), pooled[:, W * j : W * (j + 1)])
        snd[...] = packed.astype(BF16)

    def exchange_start(src, dst, ssem, rsem):
        own = rows(PACK * b, PACK)

        @pl.loop(1, NB)
        def _(i):
            to = (b + i) % NB
            rcopy(
                src.at[rows(PACK * to, PACK), :], dst.at[own, :], ssem.at[i], rsem.at[i], (to, t)
            ).start()

        dst[own, :] = src[own, :]

    def exchange_wait(src, dst, ssem, rsem):
        @pl.loop(1, NB)
        def _(i):
            to = (b + i) % NB
            came = (b + NB - i) % NB
            copy = rcopy(
                src.at[rows(PACK * to, PACK), :], dst.at[rows(PACK * came, PACK), :],
                ssem.at[i], rsem.at[i], (to, t),
            )
            copy.wait_send()
            copy.wait_recv()

    def slots():
        slot, spot = iota((2 * NB, NB * PACK), 0), iota((2 * NB, NB * PACK), 1)
        base = (slot // 2) * PACK
        arrived = arr[...]
        own = rows(2 * NB * t, 2 * NB)
        for j in range(PIECES):
            pick = onehot(spot == base + (slot % 2) * PIECES + j)
            ctx[own, W * j : W * (j + 1)] = mm(pick, arrived).astype(BF16)
        pick = onehot(spot == base + 2 * PIECES + slot % 2)
        ctx[own, E : E + FLAGS] = mm(pick, arrived[:, :FLAGS]).astype(BF16)

    def ctx_block(plane, side):
        plane = (plane + 2 * NT) % NT
        if side is None:
            return ctx.at[rows(2 * NB * plane, 2 * NB), :]
        return ctx.at[rows(2 * NB * plane + NB * side, NB), :]

    def ctx_send(step):
        cut = step == 3
        for side, sign, dev in ((0, -1, up), (1, 1, down)):
            block = ctx_block(t + sign * step, side if cut else None)
            send(block, block, c_s.at[side, step], c_r.at[side, step], dev)

    def ctx_got(step):
        cut = step == 3
        for side, sign, dev in ((0, -1, up), (1, 1, down)):
            block = ctx_block(t + sign * (step + 1), side if cut else None)
            got(block, c_s.at[side, step], c_r.at[side, step], dev)

    def latents():
        part = mm(ctx[:, :E], w_in[...]).astype(BF16)
        lat[...] = part
        wide = part.astype(F32)
        squares = wide * wide
        high = squares.astype(BF16)
        low = (squares - high.astype(F32)).astype(BF16)
        ones = jnp.ones((8, part.shape[1]), BF16)
        sqs[t] = mm_t(ones, high) + mm_t(ones, low)

        @pl.loop(1, NT)
        def _(i):
            rcopy(sqs.at[t], sqs.at[t], q_s.at[i], q_r.at[i], (b, (t + i) % NT)).start()

    def scales():
        @pl.loop(1, NT)
        def _(i):
            copy = rcopy(
                sqs.at[t], sqs.at[(t + NT - i) % NT], q_s.at[i], q_r.at[i], (b, (t + i) % NT)
            )
            copy.wait_send()
            copy.wait_recv()

        total = sqs[0]
        for i in range(1, NT):
            total = total + sqs[i]
        scale = lax.rsqrt(total / D + EPS)
        return jnp.transpose(scale)[:, 0:1]

    def project():
        scale = scales()
        for m in range(3):
            qkv[m] = (acc[m] * scale).astype(BF16)

    def head(h):
        cols = slice(DH * h, DH * (h + 1))
        seen = mm_t(jnp.ones((8, FLAGS), BF16), ctx[:, E : E + FLAGS])[0:1, :] > 0.5
        for i in range(CTX // 128):
            lines = slice(128 * i, 128 * (i + 1))
            n = 128 * (i + 1)
            scores = mm_t(qkv[0, lines, cols], qkv[1, :n, cols]) * DH ** (-0.5)
            line, place = iota((128, n), 0) + 128 * i, iota((128, n), 1)
            allowed = ((place < line) & seen[:, :n]) | (place == line)
            scores = jnp.where(allowed, scores, -1e30)
            raised = jnp.exp(scores - jnp.max(scores, axis=-1, keepdims=True))
            weights = raised / jnp.sum(raised, axis=-1, keepdims=True)
            att[lines, cols] = mm(weights.astype(BF16), qkv[2, :n, cols]).astype(BF16)

    def z_rows(plane, start, size):
        plane = (plane + 2 * NT) % NT
        return rows(2 * NB * plane + start, size)

    def z_first(n):
        value = mm(att[:, :W], m_o[n, 0]) + mm(att[:, W:], m_o[n, 1])
        zp[n] = (value + lw[:, W * n : W * (n + 1)]).astype(BF16)
        for side, dev in ((0, up), (1, down)):
            send(
                zp.at[n, z_rows(t + 4, NB * side, NB), :], zr.at[n, side, 0, pl.ds(0, NB), :],
                z_s.at[n, side, 0], z_r.at[n, side, 0], dev,
            )

    def z_add(n, step):
        for side, sign, dev in ((0, 1, up), (1, -1, down)):
            plane = t + sign * (4 - step)
            if step == 1:
                got(zr.at[n, side, 0, pl.ds(0, NB), :], z_s.at[n, side, 0], z_r.at[n, side, 0], dev)
                place, came = z_rows(plane, NB * side, NB), zr[n, side, 0, 0:NB, :]
            else:
                got(zr.at[n, side, step - 1], z_s.at[n, side, step - 1], z_r.at[n, side, step - 1], dev)
                place, came = z_rows(plane, 0, 2 * NB), zr[n, side, step - 1]
            zp[n, place, :] = (zp[n, place, :].astype(F32) + came.astype(F32)).astype(BF16)
            send(
                zp.at[n, z_rows(plane, 0, 2 * NB), :], zr.at[n, side, step],
                z_s.at[n, side, step], z_r.at[n, side, step], dev,
            )

    def z_last(n):
        total = zp[n, z_rows(t, 0, 2 * NB), :].astype(F32)
        for side, dev in ((0, up), (1, down)):
            got(zr.at[n, side, 3], z_s.at[n, side, 3], z_r.at[n, side, 3], dev)
            total = total + zr[n, side, 3].astype(F32)
        spot, slot = iota((NB * PACK, 2 * NB), 0), iota((NB * PACK, 2 * NB), 1)
        pick = onehot(spot == (slot // 2) * PACK + (slot % 2) * PIECES + n)
        term = mm(pick, total.astype(BF16))
        if n == 0:
            packf[...] = term
        else:
            packf[...] = packf[...] + term

    def decode():
        len_row, len_col, route_row, route_col, end_row, end_col, slot_row, slot_col = tables(
            lengths, route
        )
        n = states.shape[0]
        place = iota((n, lengths.shape[1]), 0).astype(F32)
        member = onehot((place >= end_row - len_row) & (place < end_row))
        spot = iota((lengths.shape[1], NB * PACK), 1).astype(F32)
        target = route_col * PACK + slot_col * PIECES
        total = jnp.zeros((n, w_head.shape[1]), F32)
        for j in range(PIECES):
            cols = slice(W * j, W * (j + 1))
            values = mm(onehot(spot == target + j), arr2[...]).astype(BF16)
            decoded = (states[:, cols].astype(F32) + mm(member, values)).astype(BF16)
            total = total + mm(decoded, w_head[cols, :])
        out[...] = total.astype(BF16)

    relay(0)
    pool()
    exchange_start(snd, arr, a_s, a_r)
    for i in range(1, STAGES + 6):
        if i < STAGES:
            relay(i)
        if i == 2:
            exchange_wait(snd, arr, a_s, a_r)
            slots()
            ctx_send(0)
        if 3 <= i <= 5:
            ctx_got(i - 3)
            ctx_send(i - 2)
        if i == 6:
            ctx_got(3)
            latents()
        if 0 <= i - 6 < STAGES:
            joined(i - 6)
        if 0 <= i - 5 < STAGES:
            second_gather(i - 5)
        if 0 <= i - 4 < STAGES:
            first_gather(i - 4)
        if 0 <= i - 3 < STAGES:
            second_sum(i - 3)
        if 0 <= i - 2 < STAGES:
            first_sum(i - 2)
        if 0 <= i - 1 < STAGES:
            product(i - 1)
        if i == 8:
            lw[...] = mm(lat[...], w_out[...])
        if i == 10:
            project()
        if 10 <= i < 14:
            head(i - 10)
        if i == 13:
            for n in range(3):
                z_first(n)
        if i == 14:
            z_first(3)
            for n in range(3):
                z_add(n, 1)
        if i == 15:
            z_first(4)
    z_add(3, 1)
    for n in range(3):
        z_add(n, 2)
    z_add(4, 1)
    z_add(3, 2)
    for n in range(3):
        z_add(n, 3)
    z_add(4, 2)
    z_add(3, 3)
    for n in range(3):
        z_last(n)
    z_add(4, 3)
    z_last(3)
    z_last(4)
    snd2[...] = packf[...].astype(BF16)
    exchange_start(snd2, arr2, b_s, b_r)
    exchange_wait(snd2, arr2, b_s, b_r)
    decode()
    for copy in sends:
        copy.wait_send()
    for j in range(STAGES):
        relay_end(j)


def body(
    byte_states, enc_gain, patch_lengths, patch_route, w_in, latent_gain,
    w_query, w_key, w_value, w_attn_out, w_out, w_head,
):
    vmem = pl.BlockSpec(memory_space=pltpu.VMEM)
    dma = pltpu.SemaphoreType.DMA
    part_q, part_o = 3 * W // 16, W // 16

    def buf(*shape, dtype=BF16):
        return pltpu.VMEM(shape, dtype)

    scratch = [
        buf(STAGES, W, W),
        buf(3, 128, 2 * W),
        buf(3, W, W),
        buf(W, W),
        buf(PIECES, 3 * W, W),
        buf(PIECES, W, W),
        buf(PIECES, 3, 4 * part_q, W),
        buf(PIECES, 3, 4 * part_o, W),
        buf(PIECES, 4 * part_q, W),
        buf(PIECES, 4 * part_o, W),
        buf(PIECES, 3, part_q, W),
        buf(PIECES, 3, part_o, W),
        buf(PIECES, 2, 3 * W, W),
        buf(PIECES, 2, W, W),
        buf(NB * PACK, W),
        buf(NB * PACK, W),
        buf(NB * PACK, W),
        buf(NB * PACK, W),
        buf(CTX, E + FLAGS),
        buf(CTX, 2 * W),
        buf(NT, 8, CTX, dtype=F32),
        buf(3, CTX, 2 * W, dtype=F32),
        buf(3, CTX, 2 * W),
        buf(CTX, 2 * W),
        buf(CTX, E, dtype=F32),
        buf(PIECES, CTX, W),
        buf(PIECES, 2, 4, 2 * NB, W),
        buf(NB * PACK, W, dtype=F32),
        dma((STAGES, 2)), dma((STAGES,)), dma((STAGES,)), dma((STAGES,)), dma((STAGES,)),
        dma((4,)), dma((4,)), dma((NB,)), dma((NB,)), dma((2, 4)), dma((2, 4)),
        dma((NT,)), dma((NT,)),
        dma((STAGES, 3)), dma((STAGES, 3)), dma((STAGES, 3)), dma((STAGES, 3)),
        dma((STAGES, 3)), dma((STAGES, 3)), dma((STAGES, 3)), dma((STAGES, 3)),
        dma((STAGES,)), dma((STAGES,)), dma((PIECES, 2, 4)), dma((PIECES, 2, 4)),
        dma((NB,)), dma((NB,)),
    ]
    return pl.pallas_call(
        kernel,
        out_shape=jax.ShapeDtypeStruct((byte_states.shape[0], w_head.shape[1]), BF16),
        in_specs=[vmem] * 12,
        out_specs=vmem,
        scratch_shapes=scratch,
        compiler_params=pltpu.CompilerParams(
            collective_id=0, has_side_effects=True, vmem_limit_bytes=56 * 1024 * 1024
        ),
    )(
        byte_states, enc_gain.reshape(1, -1), patch_lengths, patch_route.reshape(1, -1), w_in,
        latent_gain.reshape(NB, -1), w_query, w_key, w_value, w_attn_out, w_out, w_head,
    )


def solution(mesh):
    return jax.shard_map(
        body,
        mesh=mesh,
        in_specs=(
            P(("byte", "tensor"), None),
            P(),
            P(("byte", "tensor"), None),
            P(("byte", "tensor"), None, None),
            P(None, "tensor"),
            P(),
            P("byte", "tensor"),
            P("byte", "tensor"),
            P("byte", "tensor"),
            P("tensor", "byte"),
            P("tensor", None),
            P(),
        ),
        out_specs=P(("byte", "tensor"), None),
        check_vma=False,
    )
```

time: 377 us -> 168 us (0.45)
  waiting for transfers between devices: 256 us -> 0 us
  Pallas kernels: 0 us -> 165 us
  blocking collectives: 52.1 us -> 0 us
  matrix products: 26.6 us -> 0 us
  other arithmetic: 22.4 us -> 0 us
  between operations: 13.4 us -> 0.01 us
    pallas_call x0 -> x1, Pallas kernels: none -> 165 us  [body(): pl.pallas_call(kernel, out_shape=jax.ShapeDtypeStruct((byte_states.shape[...]
    reduce_scatter x2 -> x0, waiting for transfers between devices: 104 us -> none  [the longest x1 69.9 us: body(): shares = lax.psum_scatter(partial, 'byte', scatter_dimension=0, tiled=True)]
    all_gather x2 -> x0, waiting for transfers between devices: 77.9 us -> none  [the longest x1 39.4 us: body(): fused = lax.all_gather(shares, 'byte', axis=0, tiled=True)]
    psum x1 -> x0, waiting for transfers between devices: 73.5 us -> none  [body(): both = lax.psum(jnp.where(holder, both, jnp.zeros_like(both)), 'tensor')]
    all_to_all x2 -> x0, blocking collectives: 39.3 us -> none  [the longest x1 19.8 us: body(): lax.all_to_all(sending.reshape(byte_count, capacity, width), 'byte', spli...]
    dot_general x16 -> x0, matrix products: 22.9 us -> none  [the longest x8 14.1 us: dot(): return jnp.dot(a, b, preferred_element_type=jnp.float32)]
    concatenate x2 -> x0, other arithmetic: 19.4 us -> none  [the longest x1 19.4 us: body(): partial = jnp.concatenate(parts, axis=0)]
    psum x1 -> x0, blocking collectives: 12.7 us -> none  [body(): squares = lax.psum(squares, 'tensor')]
  transfers between devices with their start and end apart: 5 -> 0, of which waited for: 5 -> 0; matrix products, arithmetic and copies ran while one was open for 3% -> 0% of each run, Pallas kernels for 0% -> 0%
where the time goes in v2:
time: 168 us
  Pallas kernels  165 us (98%)
  local copies, waits for them, and re-layouts  2.86 us (2%)
    pallas_call x1, Pallas kernels, body(): pl.pallas_call(kernel, out_shape=jax.ShapeDtypeStruct((byte_states.shape[...  165 us

profile of v2, /device:TPU:1, one launch (start us, length us, event | category | flops | bytes accessed | tf_op | source)
XLA Modules:
  0.0 168.3 jit_solution(3114466392573290164)
XLA Ops:
  0.0 1.3 reshape.9.gain
  1.3 165.5 %shard_map.118 = bf16[256,256]{1,0:T(8,128)(2,1)} custom-call(bf16[256,1280]{1,0:T(8,128)(2,1)} %states.1, f32[1,1280]{1,0:T(1,128)} %reshape.9.gain, s32[1,32]{1,0:T(1,128)} %lengths.1, s32[1,32]{1,0:T(1,128)} %bitcast.3, bf16[1280,512]{1,0:T(8,128)(2,1)} %w_in.1, f32[32,128]{1,0:T(8,128)} %bitcast.2, bf16[128,512]{1,0:T(8,128)(2,1)} %w_q.1, ...), custom_call_target="tpu_custom_call" | custom-call | tf_op jit(solution)/shard_map/pallas_call | solution.py:578
  166.8 1.6 copy.14

commit v3 on v2

v3 whole, which is shorter than its diff:
```python
import jax
import jax.numpy as jnp
from jax import lax
from jax.experimental import pallas as pl
from jax.experimental.pallas import tpu as pltpu
from jax.sharding import PartitionSpec as P

MESH = pl.DeviceIdType.MESH
BF16 = jnp.bfloat16
F32 = jnp.float32
DH = 128
EPS = 1e-06
SIDE = 4
NB = 32
NT = 8
E = 1280
D = 4096
CTX = 512
W = 256
PIECES = E // W
STAGES = 2 * PIECES
FLAGS = 128
PACK = 16

ORDER = (
    ("start", 2), ("start", 3), ("start", 4), ("relay", 0, 1), ("relay", 1, 1), ("relay", 0, 2),
    ("relay", 2, 1), ("relay", 1, 2), ("exch",), ("start", 5), ("relay", 3, 1), ("relay", 0, 3),
    ("relay", 2, 2), ("relay", 4, 1), ("start", 6), ("relay", 1, 3), ("relay", 5, 1),
    ("relay", 3, 2), ("relay", 0, 4), ("relay", 2, 3), ("start", 7), ("relay", 4, 2),
    ("product", 0), ("relay", 6, 1), ("relay", 1, 4), ("relay", 5, 2), ("relay", 3, 3),
    ("start", 8), ("product", 1), ("ctx", 0), ("relay", 2, 4), ("relay", 7, 1), ("relay", 4, 3),
    ("relay", 6, 2), ("product", 2), ("turn", 0), ("start", 9), ("relay", 5, 3), ("relay", 3, 4),
    ("relay", 8, 1), ("product", 3), ("turn", 1), ("relay", 7, 2), ("relay", 4, 4), ("relay", 6, 3),
    ("relay", 9, 1), ("product", 4), ("turn", 2), ("relay", 5, 4), ("relay", 8, 2), ("product", 5),
    ("ctx", 1), ("relay", 7, 3), ("turn", 3), ("sum1", 0), ("relay", 6, 4), ("relay", 9, 2),
    ("product", 6), ("turn", 4), ("relay", 8, 3), ("sum1", 1), ("turn", 5), ("relay", 7, 4),
    ("product", 7), ("sum1", 2), ("relay", 9, 3), ("turn", 6), ("sum1", 3), ("relay", 8, 4),
    ("ctx", 2), ("product", 8), ("sum2", 0), ("sum1", 4), ("sum1", 5), ("turn", 7), ("relay", 9, 4),
    ("sum2", 1), ("product", 9), ("sum2", 2), ("sum1", 6), ("gather1", 0), ("sum2", 3), ("ctx", 3),
    ("lat",), ("turn", 8), ("sum2", 5), ("sum2", 4), ("sum1", 7), ("gather1", 1), ("turn", 9),
    ("gather1", 2), ("sum2", 6), ("gather2", 0), ("res",), ("gather1", 4), ("gather1", 3),
    ("sum1", 8), ("gather1", 5), ("sum2", 7), ("gather2", 1), ("sum1", 9), ("gather1", 6),
    ("gather2", 2), ("gather3", 0), ("gather2", 3), ("sum2", 8), ("gather2", 5), ("joined", 0),
    ("gather2", 4), ("gather1", 7), ("gather3", 1), ("sum2", 9), ("gather2", 6), ("gather3", 3),
    ("gather1", 8), ("gather3", 5), ("joined", 1), ("gather3", 2), ("gather2", 7), ("joined", 3),
    ("gather3", 4), ("joined", 5), ("gather1", 9), ("gather3", 6), ("joined", 2), ("gather2", 8),
    ("gather3", 7), ("joined", 4), ("joined", 6), ("proj",), ("gather2", 9), ("joined", 7),
    ("head", 0), ("gather3", 8), ("head", 1), ("gather3", 9), ("joined", 8), ("head", 2),
    ("joined", 9), ("head", 3), ("zf", 0), ("zf", 1), ("zf", 2), ("zf", 3), ("zf", 4), ("za", 0, 1),
    ("za", 1, 1), ("za", 2, 1), ("za", 3, 1), ("za", 4, 1), ("za", 0, 2), ("za", 1, 2),
    ("za", 2, 2), ("za", 3, 2), ("za", 4, 2), ("za", 0, 3), ("za", 1, 3), ("za", 2, 3),
    ("za", 3, 3), ("za", 4, 3), ("zl", 0), ("zl", 1), ("zl", 2), ("zl", 3), ("zl", 4),
)


def mm(a, b):
    return jnp.dot(a, b, preferred_element_type=F32)


def mm_t(a, b):
    return lax.dot_general(a, b, (((1,), (1,)), ((), ())), preferred_element_type=F32)


def iota(shape, dim):
    return lax.broadcasted_iota(jnp.int32, shape, dim)


def onehot(mask):
    return jnp.where(mask, 1.0, 0.0).astype(BF16)


def tables(lengths, route):
    n = lengths.shape[1]
    down, across = iota((n, n), 0), iota((n, n), 1)
    eye = down == across

    def column(row):
        return jnp.sum(jnp.where(eye, row, 0.0), axis=1, keepdims=True)

    len_row = lengths[...].astype(F32)
    route_row = route[...].astype(F32)
    len_col, route_col = column(len_row), column(route_row)
    end_row = jnp.sum(jnp.where(down <= across, len_col, 0.0), axis=0, keepdims=True)
    end_col = jnp.sum(jnp.where(across <= down, len_row, 0.0), axis=1, keepdims=True)
    same = jnp.where(route_row == route_col, 1.0, 0.0)
    slot_row = jnp.sum(jnp.where(down < across, same, 0.0), axis=0, keepdims=True)
    slot_col = jnp.sum(jnp.where(across < down, same, 0.0), axis=1, keepdims=True)
    return len_row, len_col, route_row, route_col, end_row, end_col, slot_row, slot_col


def kernel(
    states, gain, lengths, route, w_in, lat_gain, w_q, w_k, w_v, w_ao, w_out, w_head, out,
    blk, wsc, wx, wxo, p_q, p_o, a1_q, a1_o, b1_q, b1_o, t_q, t_o, r2_q, r2_o, m_q, m_o,
    snd, arr, snd2, arr2, ctx, lat, sqs, acc, qkv, att, lw, zp, zr, packf,
    w_s, w_r, p_s, p_r, loc, x_s, x_r, a_s, a_r, c_s, c_r, q_s, q_r,
    sum_s, a1_r, b1_r, r2_r, g1_r, g2_r, g3_r, h_r, z_s, z_r, b_s, b_r,
):
    b = lax.axis_index("byte")
    t = lax.axis_index("tensor")
    k = b % 2
    chip = b // 2
    x = chip % SIDE
    y = chip // SIDE
    far = (t - chip // 2 + NT) % NT
    up = (b, (t + 1) % NT)
    down = (b, (t + NT - 1) % NT)
    partner = (b + 1 - 2 * k, t)

    def rcopy(src, dst, ssem, rsem, dev):
        return pltpu.make_async_remote_copy(
            src_ref=src, dst_ref=dst, send_sem=ssem, recv_sem=rsem, device_id=dev, device_id_type=MESH
        )

    def send(src, dst, ssem, rsem, dev):
        rcopy(src, dst, ssem, rsem, dev).start()

    def got(dst, rsem):
        rcopy(dst, dst, rsem, rsem, partner).wait_recv()

    def sent(src, ssem):
        rcopy(src, src, ssem, ssem, partner).wait_send()

    def rows(start, size, step=16):
        return pl.ds(pl.multiple_of(start, step), size)

    bar = pltpu.get_barrier_semaphore()
    half = rows(128 * k, 128, 128)
    mine = rows(W * k, W, W)
    theirs = rows(W * (1 - k), W, W)

    def greet():
        @pl.loop(1, NB)
        def _(i):
            pl.semaphore_signal(bar, inc=1, device_id=((b + i) % NB, t), device_id_type=MESH)

        @pl.loop(1, NT)
        def _(i):
            pl.semaphore_signal(bar, inc=1, device_id=(b, (t + i) % NT), device_id_type=MESH)

    def scale_weights():
        g_row = lat_gain[pl.ds(b, 1), :]
        eye = iota((128, 128), 0) == iota((128, 128), 1)
        g_col = jnp.sum(jnp.where(eye, g_row, 0.0), axis=1, keepdims=True)
        for m, weight in enumerate((w_q, w_k, w_v)):
            wsc[m] = (weight[...].astype(F32) * g_col).astype(BF16)

    def meet():
        pl.semaphore_wait(bar, NB + NT - 2)

    def swap_weights():
        for m in range(3):
            send(wsc.at[m, :, theirs], wx.at[m, half, :], x_s.at[0], x_r.at[0], partner)
        send(w_ao.at[theirs, :], wxo.at[:, half], x_s.at[1], x_r.at[1], partner)

    off = rows(W * (chip % 2), W, W)

    def start(j):
        piece = blk.at[j, half, :]
        if j < PIECES:
            source = w_in.at[rows(W * j + 128 * k, 128, 128), off]
            whole = w_in.at[pl.ds(W * j, W), off]
        else:
            cols = pl.ds(W * (j - PIECES), W)
            source = w_out.at[rows(W * (chip % 2) + 128 * k, 128, 128), cols]
            whole = w_out.at[off, cols]

        @pl.when(far == 0)
        def _():
            send(source, piece, w_s.at[0], w_r.at[j], up)
            send(source, piece, w_s.at[1], w_r.at[j], down)
            pltpu.make_async_copy(whole, blk.at[j], loc.at[j]).start()

    def relay(j, hops):
        piece = blk.at[j, half, :]

        @pl.when(far == hops)
        def _():
            got(piece, w_r.at[j])
            if hops < NT // 2:
                send(piece, piece, w_s.at[0], w_r.at[j], up)
            send(piece, piece, p_s, p_r.at[j], partner)

        if hops < NT // 2:

            @pl.when(far == NT - hops)
            def _():
                got(piece, w_r.at[j])
                if hops < NT // 2 - 1:
                    send(piece, piece, w_s.at[1], w_r.at[j], down)
                send(piece, piece, p_s, p_r.at[j], partner)

    def relay_end():
        pieces = blk.at[:, half, :]

        @pl.when(far <= 3)
        def _():
            sent(pieces, w_s.at[0])

        @pl.when((far == 0) | (far >= 6))
        def _():
            sent(pieces, w_s.at[1])

        @pl.when(far != 0)
        def _():
            sent(pieces, p_s)

    def layout(j):
        if j < PIECES:
            return j, 3 * W // 16, (p_q, a1_q, b1_q, t_q, r2_q, m_q), 0
        return j - PIECES, W // 16, (p_o, a1_o, b1_o, t_o, r2_o, m_o), 1

    def axes(j):
        return (x, y) if j % 2 == 0 else (y, x)

    def peer(j, first, i):
        along_x = (j % 2 == 0) == first
        px = (x + i) % SIDE if along_x else x
        py = y if along_x else (y + i) % SIDE
        return ((py * SIDE + px) * 2 + k, t)

    def product(j):
        other = rows(128 * (1 - k), 128, 128)

        @pl.when(far == 0)
        def _():
            pltpu.make_async_copy(blk.at[j], blk.at[j], loc.at[j]).wait()

        @pl.when(far != 0)
        def _():
            got(blk.at[j, other, :], p_r.at[j])

        if j == 0:
            got(wx.at[:, other, :], x_r.at[0])
            for m in range(3):
                wx[m, half, :] = wsc[m, :, mine]
        if j == PIECES:
            got(wxo.at[:, other], x_r.at[1])
            wxo[:, half] = w_ao[mine, :]
        n, part, (p, a1, b1, tt, r2, m_), kind = layout(j)
        if j < PIECES:
            for m in range(3):
                p[n, W * m : W * (m + 1), :] = mm(blk[j], wx[m]).astype(BF16)
        else:
            p[n] = mm(wxo[...], blk[j]).astype(BF16)
        u, v = axes(j)
        for side, way in ((0, 1), (1, SIDE - 1)):
            block = rows(4 * part * ((u + 2) % SIDE) + 2 * part * side, 2 * part)
            send(
                p.at[n, block, :], a1.at[n, side],
                sum_s.at[0, kind], a1_r.at[j], peer(j, True, way),
            )

    def turn(j):
        n, part, (p, a1, b1, tt, r2, m_), kind = layout(j)
        u, v = axes(j)
        got(a1.at[n], a1_r.at[j])
        for side, way in ((0, 1), (1, SIDE - 1)):
            base = 4 * part * ((u + way) % SIDE)
            cut = rows(base + 2 * part * side, 2 * part)
            p[n, cut, :] = (p[n, cut, :].astype(F32) + a1[n, side].astype(F32)).astype(BF16)
            send(
                p.at[n, rows(base, 4 * part), :], b1.at[n, side],
                sum_s.at[1, kind], b1_r.at[j], peer(j, True, way),
            )

    def sum1(j):
        n, part, (p, a1, b1, tt, r2, m_), kind = layout(j)
        u, v = axes(j)
        got(b1.at[n], b1_r.at[j])
        total = p[n, rows(4 * part * u, 4 * part), :].astype(F32)
        total = total + b1[n, 0].astype(F32) + b1[n, 1].astype(F32)
        tt[n] = total.astype(BF16)
        for i in range(1, SIDE):
            to = (v + i) % SIDE
            send(
                tt.at[n, rows(part * to, part), :], r2.at[n, i - 1],
                sum_s.at[2, kind], r2_r.at[j], peer(j, False, i),
            )

    def sum2(j):
        n, part, (p, a1, b1, tt, r2, m_), kind = layout(j)
        u, v = axes(j)
        got(r2.at[n], r2_r.at[j])
        total = tt[n, rows(part * v, part), :].astype(F32)
        for i in range(SIDE - 1):
            total = total + r2[n, i].astype(F32)
        own = rows(part * (4 * u + v), part)
        m_[n, k, own, :] = total.astype(BF16)
        for i in range(1, SIDE):
            send(
                m_.at[n, k, own, :], m_.at[n, k, own, :],
                sum_s.at[3, kind], g1_r.at[j], peer(j, False, i),
            )

    def gather1(j):
        n, part, (p, a1, b1, tt, r2, m_), kind = layout(j)
        u, v = axes(j)
        got(r2.at[n], g1_r.at[j])
        own = rows(4 * part * u, 4 * part)
        for way in (1, SIDE - 1):
            send(
                m_.at[n, k, own, :], m_.at[n, k, own, :],
                sum_s.at[4, kind], g2_r.at[j], peer(j, True, way),
            )

    def gather2(j):
        n, part, (p, a1, b1, tt, r2, m_), kind = layout(j)
        u, v = axes(j)
        got(b1.at[n], g2_r.at[j])
        for side, way in ((0, 1), (1, SIDE - 1)):
            base = 4 * part * ((u + SIDE - way) % SIDE) + 2 * part * side
            block = m_.at[n, k, rows(base, 2 * part), :]
            send(block, block, sum_s.at[5, kind], g3_r.at[j], peer(j, True, way))

    def gather3(j):
        n, part, (p, a1, b1, tt, r2, m_), kind = layout(j)
        got(a1.at[n], g3_r.at[j])
        send(m_.at[n, k], m_.at[n, k], sum_s.at[6, kind], h_r.at[j], partner)

    def joined(j):
        n, part, (p, a1, b1, tt, r2, m_), kind = layout(j)
        got(m_.at[n, 1 - k], h_r.at[j])
        if j < PIECES:
            piece = ctx[:, W * j : W * (j + 1)]
            for m in range(3):
                for side in range(2):
                    cols = slice(W * side, W * (side + 1))
                    term = mm(piece, m_[n, side, W * m : W * (m + 1), :])
                    if j == 0:
                        acc[m, :, cols] = term
                    else:
                        acc[m, :, cols] = acc[m, :, cols] + term

    def sums_end():
        for kind in range(2):
            p, a1, b1, tt, r2, m_ = layout(kind * PIECES)[2]
            for i, ref in enumerate((a1, b1, r2, r2, b1, a1)):
                sent(ref, sum_s.at[i, kind])
            sent(m_.at[:, 0], sum_s.at[6, kind])

    def pool():
        len_row, len_col, route_row, route_col, end_row, end_col, slot_row, slot_col = tables(
            lengths, route
        )
        values = states[...].astype(F32)
        scale = lax.rsqrt(jnp.mean(values * values, axis=-1, keepdims=True) + EPS)
        normed = values * scale * gain[...]
        high = normed.astype(BF16)
        low = (normed - high.astype(F32)).astype(BF16)
        n = states.shape[0]
        place = iota((lengths.shape[1], n), 1).astype(F32)
        member = onehot((place >= end_col - len_col) & (place < end_col))
        pooled = ((mm(member, high) + mm(member, low)) / len_col).astype(BF16)
        spot = iota((NB * PACK, lengths.shape[1]), 0).astype(F32)
        target = route_row * PACK + slot_row * PIECES
        packed = mm(
            onehot(spot == route_row * PACK + 2 * PIECES + slot_row),
            jnp.ones((lengths.shape[1], W), BF16),
        )
        for j in range(PIECES):
            packed = packed + mm(onehot(spot == target + j), pooled[:, W * j : W * (j + 1)])
        snd[...] = packed.astype(BF16)

    def exchange_start(src, dst, ssem, rsem):
        own = rows(PACK * b, PACK)

        @pl.loop(1, NB)
        def _(i):
            to = (b + i) % NB
            send(src.at[rows(PACK * to, PACK), :], dst.at[own, :], ssem, rsem, (to, t))

        dst[own, :] = src[own, :]

    def exchange_wait(src, dst, ssem, rsem):
        most = pl.ds(0, (NB - 1) * PACK)
        sent(src.at[most, :], ssem)
        got(dst.at[most, :], rsem)

    def slots():
        slot, spot = iota((2 * NB, NB * PACK), 0), iota((2 * NB, NB * PACK), 1)
        base = (slot // 2) * PACK
        arrived = arr[...]
        own = rows(2 * NB * t, 2 * NB)
        for j in range(PIECES):
            pick = onehot(spot == base + (slot % 2) * PIECES + j)
            ctx[own, W * j : W * (j + 1)] = mm(pick, arrived).astype(BF16)
        pick = onehot(spot == base + 2 * PIECES + slot % 2)
        ctx[own, E : E + FLAGS] = mm(pick, arrived[:, :FLAGS]).astype(BF16)

    def ctx_block(plane, side):
        plane = (plane + 2 * NT) % NT
        if side is None:
            return ctx.at[rows(2 * NB * plane, 2 * NB), :]
        return ctx.at[rows(2 * NB * plane + NB * side, NB), :]

    def ctx_send(step):
        cut = step == 3
        for side, sign, dev in ((0, -1, up), (1, 1, down)):
            block = ctx_block(t + sign * step, side if cut else None)
            send(block, block, c_s.at[side], c_r.at[side, step], dev)

    def ctx_got(step):
        cut = step == 3
        for side, sign, dev in ((0, -1, up), (1, 1, down)):
            block = ctx_block(t + sign * (step + 1), side if cut else None)
            got(block, c_r.at[side, step])

    def ctx_end():
        for side in range(2):
            sent(ctx.at[pl.ds(0, 7 * NB), :], c_s.at[side])

    def latents():
        part = mm(ctx[:, :E], w_in[...]).astype(BF16)
        lat[...] = part
        wide = part.astype(F32)
        squares = wide * wide
        high = squares.astype(BF16)
        low = (squares - high.astype(F32)).astype(BF16)
        ones = jnp.ones((8, part.shape[1]), BF16)
        sqs[t] = mm_t(ones, high) + mm_t(ones, low)

        @pl.loop(1, NT)
        def _(i):
            send(sqs.at[t], sqs.at[t], q_s, q_r, (b, (t + i) % NT))

    def scales():
        most = sqs.at[pl.ds(0, NT - 1)]
        sent(most, q_s)
        got(most, q_r)
        total = sqs[0]
        for i in range(1, NT):
            total = total + sqs[i]
        scale = lax.rsqrt(total / D + EPS)
        return jnp.transpose(scale)[:, 0:1]

    def project():
        scale = scales()
        for m in range(3):
            qkv[m] = (acc[m] * scale).astype(BF16)

    def head(h):
        cols = slice(DH * h, DH * (h + 1))
        seen = mm_t(jnp.ones((8, FLAGS), BF16), ctx[:, E : E + FLAGS])[0:1, :] > 0.5
        for i in range(CTX // 128):
            lines = slice(128 * i, 128 * (i + 1))
            n = 128 * (i + 1)
            scores = mm_t(qkv[0, lines, cols], qkv[1, :n, cols]) * DH ** (-0.5)
            line, place = iota((128, n), 0) + 128 * i, iota((128, n), 1)
            allowed = ((place < line) & seen[:, :n]) | (place == line)
            scores = jnp.where(allowed, scores, -1e30)
            raised = jnp.exp(scores - jnp.max(scores, axis=-1, keepdims=True))
            weights = raised / jnp.sum(raised, axis=-1, keepdims=True)
            att[lines, cols] = mm(weights.astype(BF16), qkv[2, :n, cols]).astype(BF16)

    def z_rows(plane, start, size):
        plane = (plane + 2 * NT) % NT
        return rows(2 * NB * plane + start, size)

    def z_first(n):
        value = mm(att[:, :W], m_o[n, 0]) + mm(att[:, W:], m_o[n, 1])
        zp[n] = (value + lw[:, W * n : W * (n + 1)]).astype(BF16)
        for side, dev in ((0, up), (1, down)):
            send(
                zp.at[n, z_rows(t + 4, NB * side, NB), :], zr.at[n, 0, side, pl.ds(0, NB), :],
                z_s.at[0], z_r.at[n, 0], dev,
            )

    def z_add(n, step):
        if step == 1:
            got(zr.at[n, 0, :, pl.ds(0, NB), :], z_r.at[n, 0])
        else:
            got(zr.at[n, step - 1], z_r.at[n, step - 1])
        for side, sign, dev in ((0, 1, up), (1, -1, down)):
            plane = t + sign * (4 - step)
            if step == 1:
                place, came = z_rows(plane, NB * side, NB), zr[n, 0, side, 0:NB, :]
            else:
                place, came = z_rows(plane, 0, 2 * NB), zr[n, step - 1, side]
            zp[n, place, :] = (zp[n, place, :].astype(F32) + came.astype(F32)).astype(BF16)
            send(
                zp.at[n, z_rows(plane, 0, 2 * NB), :], zr.at[n, step, side],
                z_s.at[1], z_r.at[n, step], dev,
            )

    def z_last(n):
        got(zr.at[n, 3], z_r.at[n, 3])
        total = zp[n, z_rows(t, 0, 2 * NB), :].astype(F32)
        total = total + zr[n, 3, 0].astype(F32) + zr[n, 3, 1].astype(F32)
        spot, slot = iota((NB * PACK, 2 * NB), 0), iota((NB * PACK, 2 * NB), 1)
        pick = onehot(spot == (slot // 2) * PACK + (slot % 2) * PIECES + n)
        term = mm(pick, total.astype(BF16))
        if n == 0:
            packf[...] = term
        else:
            packf[...] = packf[...] + term

    def z_end():
        sent(zr.at[:, 0, :, pl.ds(0, NB), :], z_s.at[0])
        sent(zr.at[:, pl.ds(1, 3)], z_s.at[1])

    def decode():
        len_row, len_col, route_row, route_col, end_row, end_col, slot_row, slot_col = tables(
            lengths, route
        )
        n = states.shape[0]
        place = iota((n, lengths.shape[1]), 0).astype(F32)
        member = onehot((place >= end_row - len_row) & (place < end_row))
        spot = iota((lengths.shape[1], NB * PACK), 1).astype(F32)
        target = route_col * PACK + slot_col * PIECES
        total = jnp.zeros((n, w_head.shape[1]), F32)
        for j in range(PIECES):
            cols = slice(W * j, W * (j + 1))
            values = mm(onehot(spot == target + j), arr2[...]).astype(BF16)
            decoded = (states[:, cols].astype(F32) + mm(member, values)).astype(BF16)
            total = total + mm(decoded, w_head[cols, :])
        out[...] = total.astype(BF16)

    def add_residual():
        lw[...] = mm(lat[...], w_out[...])

    def exch():
        exchange_wait(snd, arr, a_s, a_r)
        slots()
        ctx_send(0)

    def ctx_step(step):
        ctx_got(step)
        if step < 3:
            ctx_send(step + 1)

    def finish():
        sent(wsc.at[:, :, theirs], x_s.at[0])
        sent(wxo.at[:, half], x_s.at[1])
        relay_end()
        ctx_end()
        sums_end()
        z_end()

    stages = {
        "start": start, "relay": relay, "product": product, "turn": turn, "sum1": sum1,
        "sum2": sum2, "gather1": gather1, "gather2": gather2, "gather3": gather3,
        "joined": joined, "exch": exch, "ctx": ctx_step, "lat": latents, "res": add_residual,
        "proj": project, "head": head, "zf": z_first, "za": z_add, "zl": z_last,
    }
    greet()
    scale_weights()
    pool()
    meet()
    swap_weights()
    start(0)
    start(1)
    exchange_start(snd, arr, a_s, a_r)
    for name, *where in ORDER:
        stages[name](*where)
    snd2[...] = packf[...].astype(BF16)
    exchange_start(snd2, arr2, b_s, b_r)
    exchange_wait(snd2, arr2, b_s, b_r)
    decode()
    finish()


def body(
    byte_states, enc_gain, patch_lengths, patch_route, w_in, latent_gain,
    w_query, w_key, w_value, w_attn_out, w_out, w_head,
):
    vmem = pl.BlockSpec(memory_space=pltpu.VMEM)
    dma = pltpu.SemaphoreType.DMA
    part_q, part_o = 3 * W // 16, W // 16

    def buf(*shape, dtype=BF16):
        return pltpu.VMEM(shape, dtype)

    scratch = [
        buf(STAGES, W, W),
        buf(3, 128, 2 * W),
        buf(3, W, W),
        buf(W, W),
        buf(PIECES, 3 * W, W),
        buf(PIECES, W, W),
        buf(PIECES, 2, 2 * part_q, W),
        buf(PIECES, 2, 2 * part_o, W),
        buf(PIECES, 2, 4 * part_q, W),
        buf(PIECES, 2, 4 * part_o, W),
        buf(PIECES, 4 * part_q, W),
        buf(PIECES, 4 * part_o, W),
        buf(PIECES, 3, part_q, W),
        buf(PIECES, 3, part_o, W),
        buf(PIECES, 2, 3 * W, W),
        buf(PIECES, 2, W, W),
        buf(NB * PACK, W),
        buf(NB * PACK, W),
        buf(NB * PACK, W),
        buf(NB * PACK, W),
        buf(CTX, E + FLAGS),
        buf(CTX, 2 * W),
        buf(NT, 8, CTX, dtype=F32),
        buf(3, CTX, 2 * W, dtype=F32),
        buf(3, CTX, 2 * W),
        buf(CTX, 2 * W),
        buf(CTX, E, dtype=F32),
        buf(PIECES, CTX, W),
        buf(PIECES, 4, 2, 2 * NB, W),
        buf(NB * PACK, W, dtype=F32),
        dma((2,)), dma((STAGES,)), dma, dma((STAGES,)), dma((STAGES,)),
        dma((2,)), dma((2,)), dma, dma, dma((2,)), dma((2, 4)), dma, dma,
        dma((7, 2)),
        dma((STAGES,)), dma((STAGES,)), dma((STAGES,)), dma((STAGES,)), dma((STAGES,)),
        dma((STAGES,)), dma((STAGES,)),
        dma((2,)), dma((PIECES, 4)), dma, dma,
    ]
    return pl.pallas_call(
        kernel,
        out_shape=jax.ShapeDtypeStruct((byte_states.shape[0], w_head.shape[1]), BF16),
        in_specs=[vmem] * 12,
        out_specs=vmem,
        scratch_shapes=scratch,
        compiler_params=pltpu.CompilerParams(
            collective_id=0, has_side_effects=True, vmem_limit_bytes=56 * 1024 * 1024
        ),
    )(
        byte_states, enc_gain.reshape(1, -1), patch_lengths, patch_route.reshape(1, -1), w_in,
        latent_gain.reshape(NB, -1), w_query, w_key, w_value, w_attn_out, w_out, w_head,
    )


def solution(mesh):
    return jax.shard_map(
        body,
        mesh=mesh,
        in_specs=(
            P(("byte", "tensor"), None),
            P(),
            P(("byte", "tensor"), None),
            P(("byte", "tensor"), None, None),
            P(None, "tensor"),
            P(),
            P("byte", "tensor"),
            P("byte", "tensor"),
            P("byte", "tensor"),
            P("tensor", "byte"),
            P("tensor", None),
            P(),
        ),
        out_specs=P(("byte", "tensor"), None),
        check_vma=False,
    )
```

time: 168 us -> 112 us (0.67)
  Pallas kernels: 165 us -> 109 us
    pallas_call x1, Pallas kernels: 165 us -> 109 us  [body(): pl.pallas_call(kernel, out_shape=jax.ShapeDtypeStruct((byte_states.shape[...]
where the time goes in v3:
time: 112 us
  Pallas kernels  109 us (97%)
  local copies, waits for them, and re-layouts  2.86 us (3%)
    pallas_call x1, Pallas kernels, body(): pl.pallas_call(kernel, out_shape=jax.ShapeDtypeStruct((byte_states.shape[...  109 us

profile of v3, /device:TPU:1, one launch (start us, length us, event | category | flops | bytes accessed | tf_op | source)
XLA Modules:
  0.0 112.3 jit_solution(16526356193072823277)
XLA Ops:
  0.0 1.3 %reshape.9.gain = f32[1,1280]{1,0:T(1,128)} reshape(f32[1280]{0:T(1024)} %param.13) | data formatting | bytes 10240 | tf_op jit(solution)/shard_map/reshape | solution.py:621
  1.3 109.4 %shard_map.118 = bf16[256,256]{1,0:T(8,128)(2,1)} custom-call(bf16[256,1280]{1,0:T(8,128)(2,1)} %states.1, f32[1,1280]{1,0:T(1,128)} %reshape.9.gain, s32[1,32]{1,0:T(1,128)} %lengths.1, s32[1,32]{1,0:T(1,128)} %bitcast.3, bf16[1280,512]{1,0:T(8,128)(2,1)} %w_in.1, f32[32,128]{1,0:T(8,128)} %bitcast.2, bf16[128,512]{1,0:T(8,128)(2,1)} %w_q.1, ...), custom_call_target="tpu_custom_call" | custom-call | tf_op jit(solution)/shard_map/pallas_call | solution.py:611
  110.7 1.6 %copy.14 = bf16[256,256]{1,0:T(8,128)(2,1)} copy(bf16[256,256]{1,0:T(8,128)(2,1)} %shard_map.118) | data formatting | bytes 262144

commit v4 on v3

--- a/solution.py
+++ b/solution.py
@@ -10,6 +10,7 @@
 F32 = jnp.float32
 DH = 128
 EPS = 1e-06
+LOG2E = 1.4426950408889634
 SIDE = 4
 NB = 32
 NT = 8
@@ -24,32 +25,32 @@
 
 ORDER = (
     ("start", 2), ("start", 3), ("start", 4), ("relay", 0, 1), ("relay", 1, 1), ("relay", 0, 2),
-    ("relay", 2, 1), ("relay", 1, 2), ("exch",), ("start", 5), ("relay", 3, 1), ("relay", 0, 3),
-    ("relay", 2, 2), ("relay", 4, 1), ("start", 6), ("relay", 1, 3), ("relay", 5, 1),
-    ("relay", 3, 2), ("relay", 0, 4), ("relay", 2, 3), ("start", 7), ("relay", 4, 2),
-    ("product", 0), ("relay", 6, 1), ("relay", 1, 4), ("relay", 5, 2), ("relay", 3, 3),
-    ("start", 8), ("product", 1), ("ctx", 0), ("relay", 2, 4), ("relay", 7, 1), ("relay", 4, 3),
-    ("relay", 6, 2), ("product", 2), ("turn", 0), ("start", 9), ("relay", 5, 3), ("relay", 3, 4),
-    ("relay", 8, 1), ("product", 3), ("turn", 1), ("relay", 7, 2), ("relay", 4, 4), ("relay", 6, 3),
-    ("relay", 9, 1), ("product", 4), ("turn", 2), ("relay", 5, 4), ("relay", 8, 2), ("product", 5),
-    ("ctx", 1), ("relay", 7, 3), ("turn", 3), ("sum1", 0), ("relay", 6, 4), ("relay", 9, 2),
-    ("product", 6), ("turn", 4), ("relay", 8, 3), ("sum1", 1), ("turn", 5), ("relay", 7, 4),
-    ("product", 7), ("sum1", 2), ("relay", 9, 3), ("turn", 6), ("sum1", 3), ("relay", 8, 4),
-    ("ctx", 2), ("product", 8), ("sum2", 0), ("sum1", 4), ("sum1", 5), ("turn", 7), ("relay", 9, 4),
-    ("sum2", 1), ("product", 9), ("sum2", 2), ("sum1", 6), ("gather1", 0), ("sum2", 3), ("ctx", 3),
-    ("lat",), ("turn", 8), ("sum2", 5), ("sum2", 4), ("sum1", 7), ("gather1", 1), ("turn", 9),
-    ("gather1", 2), ("sum2", 6), ("gather2", 0), ("res",), ("gather1", 4), ("gather1", 3),
-    ("sum1", 8), ("gather1", 5), ("sum2", 7), ("gather2", 1), ("sum1", 9), ("gather1", 6),
-    ("gather2", 2), ("gather3", 0), ("gather2", 3), ("sum2", 8), ("gather2", 5), ("joined", 0),
-    ("gather2", 4), ("gather1", 7), ("gather3", 1), ("sum2", 9), ("gather2", 6), ("gather3", 3),
-    ("gather1", 8), ("gather3", 5), ("joined", 1), ("gather3", 2), ("gather2", 7), ("joined", 3),
-    ("gather3", 4), ("joined", 5), ("gather1", 9), ("gather3", 6), ("joined", 2), ("gather2", 8),
-    ("gather3", 7), ("joined", 4), ("joined", 6), ("proj",), ("gather2", 9), ("joined", 7),
-    ("head", 0), ("gather3", 8), ("head", 1), ("gather3", 9), ("joined", 8), ("head", 2),
-    ("joined", 9), ("head", 3), ("zf", 0), ("zf", 1), ("zf", 2), ("zf", 3), ("zf", 4), ("za", 0, 1),
-    ("za", 1, 1), ("za", 2, 1), ("za", 3, 1), ("za", 4, 1), ("za", 0, 2), ("za", 1, 2),
-    ("za", 2, 2), ("za", 3, 2), ("za", 4, 2), ("za", 0, 3), ("za", 1, 3), ("za", 2, 3),
-    ("za", 3, 3), ("za", 4, 3), ("zl", 0), ("zl", 1), ("zl", 2), ("zl", 3), ("zl", 4),
+    ("relay", 2, 1), ("relay", 1, 2), ("relay", 3, 1), ("exch",), ("relay", 0, 3), ("start", 5),
+    ("relay", 2, 2), ("relay", 4, 1), ("relay", 1, 3), ("start", 6), ("relay", 3, 2),
+    ("relay", 0, 4), ("relay", 5, 1), ("relay", 2, 3), ("start", 7), ("relay", 4, 2),
+    ("product", 0), ("relay", 1, 4), ("relay", 6, 1), ("relay", 3, 3), ("start", 8), ("product", 1),
+    ("relay", 5, 2), ("relay", 2, 4), ("relay", 7, 1), ("relay", 4, 3), ("product", 2),
+    ("start", 9), ("relay", 6, 2), ("relay", 3, 4), ("turn", 0), ("relay", 8, 1), ("relay", 5, 3),
+    ("product", 3), ("relay", 7, 2), ("relay", 4, 4), ("turn", 1), ("relay", 9, 1), ("relay", 6, 3),
+    ("product", 4), ("relay", 8, 2), ("turn", 2), ("relay", 5, 4), ("relay", 7, 3), ("relay", 9, 2),
+    ("turn", 3), ("relay", 6, 4), ("product", 5), ("sum1", 0), ("relay", 8, 3), ("turn", 4),
+    ("relay", 7, 4), ("product", 6), ("sum1", 1), ("relay", 9, 3), ("ctxgo",), ("relay", 8, 4),
+    ("product", 7), ("sum1", 2), ("sum1", 3), ("relay", 9, 4), ("product", 8), ("sum1", 5),
+    ("ctx", 0, 0), ("sum1", 4), ("product", 9), ("sum2", 0), ("sum1", 6), ("ctx", 0, 1),
+    ("sum1", 7), ("sum2", 1), ("own",), ("sum2", 2), ("sum2", 3), ("ctx", 1, 0), ("sum2", 4),
+    ("sum1", 8), ("sum2", 5), ("sum2", 7), ("ctx", 1, 1), ("sum1", 9), ("gather1", 1),
+    ("gather1", 0), ("sum2", 6), ("gather1", 3), ("gather1", 5), ("ctx", 2, 0), ("gather1", 2),
+    ("gather1", 7), ("gather1", 4), ("sum2", 8), ("sum2", 9), ("ctx", 2, 1), ("ctx", 3, 0),
+    ("gather2", 1), ("gather2", 0), ("gather1", 6), ("ctx", 3, 1), ("gather2", 2), ("gather2", 3),
+    ("lat",), ("mask",), ("gather3", 5), ("gather2", 4), ("gather1", 9), ("gather3", 7),
+    ("gather1", 8), ("gather3", 0), ("joined", 5), ("joined", 7), ("gather3", 1), ("res",),
+    ("gather3", 6), ("gather3", 3), ("joined", 0), ("gather3", 2), ("joined", 1), ("gather3", 9),
+    ("gather3", 4), ("joined", 6), ("joined", 3), ("gather3", 8), ("joined", 2), ("joined", 9),
+    ("joined", 4), ("joined", 8), ("proj",), ("head", 0), ("head", 1), ("head", 2), ("head", 3),
+    ("zf", 0), ("zf", 1), ("zf", 2), ("zf", 3), ("zf", 4), ("za", 0, 1), ("za", 1, 1), ("za", 2, 1),
+    ("za", 3, 1), ("za", 4, 1), ("za", 0, 2), ("za", 1, 2), ("za", 2, 2), ("za", 3, 2),
+    ("za", 4, 2), ("za", 0, 3), ("za", 1, 3), ("za", 2, 3), ("za", 3, 3), ("za", 4, 3), ("zl", 0),
+    ("zl", 1), ("zl", 2), ("zl", 3), ("zl", 4),
 )
 
 
@@ -89,9 +90,11 @@
 
 
 def kernel(
-    states, gain, lengths, route, w_in, lat_gain, w_q, w_k, w_v, w_ao, w_out, w_head, out,
-    blk, wsc, wx, wxo, p_q, p_o, a1_q, a1_o, b1_q, b1_o, t_q, t_o, r2_q, r2_o, m_q, m_o,
-    snd, arr, snd2, arr2, ctx, lat, sqs, acc, qkv, att, lw, zp, zr, packf,
+    states_far, gain_far, lengths_far, route_far, w_in_far, lat_gain_far,
+    w_q_far, w_k_far, w_v_far, w_ao_far, w_out_far, w_head_far, out,
+    states, gain, lengths, route, w_in, lat_gain, w_q, w_k, w_v, w_ao, w_out, w_head, in_s,
+    blk, wsc, wx, wxo, p_q, p_o, a1_q, b1_q, r1_o, t_q, t_o, r2_q, r2_o, m_q, m_o,
+    snd, arr, snd2, arr2, ctx, lat, sqs, acc, qk, vals, bias, base, att, lw, zp, zr, packf,
     w_s, w_r, p_s, p_r, loc, x_s, x_r, a_s, a_r, c_s, c_r, q_s, q_r,
     sum_s, a1_r, b1_r, r2_r, g1_r, g2_r, g3_r, h_r, z_s, z_r, b_s, b_r,
 ):
@@ -144,6 +147,23 @@
         for m, weight in enumerate((w_q, w_k, w_v)):
             wsc[m] = (weight[...].astype(F32) * g_col).astype(BF16)
 
+    loads = {
+        "gain": (lat_gain_far, lat_gain), "scale": (gain_far, gain), "lengths": (lengths_far, lengths),
+        "route": (route_far, route), "states": (states_far, states), "q": (w_q_far, w_q),
+        "k": (w_k_far, w_k), "v": (w_v_far, w_v), "ao": (w_ao_far, w_ao), "in": (w_in_far, w_in),
+        "out": (w_out_far, w_out), "head": (w_head_far, w_head),
+    }
+    places = {name: i for i, name in enumerate(loads)}
+
+    def load_start():
+        for name, (src, dst) in loads.items():
+            pltpu.make_async_copy(src, dst, in_s.at[places[name]]).start()
+
+    def load_wait(*names):
+        for name in names:
+            src, dst = loads[name]
+            pltpu.make_async_copy(src, dst, in_s.at[places[name]]).wait()
+
     def meet():
         pl.semaphore_wait(bar, NB + NT - 2)
 
@@ -154,40 +174,49 @@
 
     off = rows(W * (chip % 2), W, W)
 
+    def cuts(j):
+        return [rows(128 * k + 64 * i, 64, 64) for i in range(2)]
+
     def start(j):
-        piece = blk.at[j, half, :]
         if j < PIECES:
-            source = w_in.at[rows(W * j + 128 * k, 128, 128), off]
-            whole = w_in.at[pl.ds(W * j, W), off]
+            whole = w_in_far.at[pl.ds(W * j, W), off]
         else:
-            cols = pl.ds(W * (j - PIECES), W)
-            source = w_out.at[rows(W * (chip % 2) + 128 * k, 128, 128), cols]
-            whole = w_out.at[off, cols]
+            whole = w_out_far.at[off, pl.ds(W * (j - PIECES), W)]
 
         @pl.when(far == 0)
         def _():
-            send(source, piece, w_s.at[0], w_r.at[j], up)
-            send(source, piece, w_s.at[1], w_r.at[j], down)
+            for i, cut in enumerate(cuts(j)):
+                if j < PIECES:
+                    source = w_in_far.at[rows(W * j + 128 * k + 64 * i, 64, 64), off]
+                else:
+                    cols = pl.ds(W * (j - PIECES), W)
+                    source = w_out_far.at[rows(W * (chip % 2) + 128 * k + 64 * i, 64, 64), cols]
+                send(source, blk.at[j, cut, :], w_s.at[0], w_r.at[j, i], up)
+                send(source, blk.at[j, cut, :], w_s.at[1], w_r.at[j, i], down)
             pltpu.make_async_copy(whole, blk.at[j], loc.at[j]).start()
 
     def relay(j, hops):
-        piece = blk.at[j, half, :]
+        last = NT // 2
 
         @pl.when(far == hops)
         def _():
-            got(piece, w_r.at[j])
-            if hops < NT // 2:
-                send(piece, piece, w_s.at[0], w_r.at[j], up)
-            send(piece, piece, p_s, p_r.at[j], partner)
-
-        if hops < NT // 2:
+            for i, cut in enumerate(cuts(j)):
+                piece = blk.at[j, cut, :]
+                got(piece, w_r.at[j, i])
+                if hops < last:
+                    send(piece, piece, w_s.at[0], w_r.at[j, i], up)
+                send(piece, piece, p_s, p_r.at[j], partner)
+
+        if hops < last:
 
             @pl.when(far == NT - hops)
             def _():
-                got(piece, w_r.at[j])
-                if hops < NT // 2 - 1:
-                    send(piece, piece, w_s.at[1], w_r.at[j], down)
-                send(piece, piece, p_s, p_r.at[j], partner)
+                for i, cut in enumerate(cuts(j)):
+                    piece = blk.at[j, cut, :]
+                    got(piece, w_r.at[j, i])
+                    if hops < last - 1:
+                        send(piece, piece, w_s.at[1], w_r.at[j, i], down)
+                    send(piece, piece, p_s, p_r.at[j], partner)
 
     def relay_end():
         pieces = blk.at[:, half, :]
@@ -206,8 +235,8 @@
 
     def layout(j):
         if j < PIECES:
-            return j, 3 * W // 16, (p_q, a1_q, b1_q, t_q, r2_q, m_q), 0
-        return j - PIECES, W // 16, (p_o, a1_o, b1_o, t_o, r2_o, m_o), 1
+            return j, 3 * W // 16, (p_q, t_q, r2_q, m_q), 0
+        return j - PIECES, W // 16, (p_o, t_o, r2_o, m_o), 1
 
     def axes(j):
         return (x, y) if j % 2 == 0 else (y, x)
@@ -236,39 +265,51 @@
         if j == PIECES:
             got(wxo.at[:, other], x_r.at[1])
             wxo[:, half] = w_ao[mine, :]
-        n, part, (p, a1, b1, tt, r2, m_), kind = layout(j)
+        n, part, (p, tt, r2, m_), kind = layout(j)
         if j < PIECES:
             for m in range(3):
                 p[n, W * m : W * (m + 1), :] = mm(blk[j], wx[m]).astype(BF16)
         else:
             p[n] = mm(wxo[...], blk[j]).astype(BF16)
         u, v = axes(j)
+        if kind:
+            for i in range(1, SIDE):
+                block = rows(4 * part * ((u + i) % SIDE), 4 * part)
+                send(
+                    p.at[n, block, :], r1_o.at[n, i - 1],
+                    sum_s.at[0, kind], a1_r.at[j], peer(j, True, i),
+                )
+            return
         for side, way in ((0, 1), (1, SIDE - 1)):
             block = rows(4 * part * ((u + 2) % SIDE) + 2 * part * side, 2 * part)
             send(
-                p.at[n, block, :], a1.at[n, side],
+                p.at[n, block, :], a1_q.at[n, side],
                 sum_s.at[0, kind], a1_r.at[j], peer(j, True, way),
             )
 
     def turn(j):
-        n, part, (p, a1, b1, tt, r2, m_), kind = layout(j)
+        n, part, (p, tt, r2, m_), kind = layout(j)
         u, v = axes(j)
-        got(a1.at[n], a1_r.at[j])
+        got(a1_q.at[n], a1_r.at[j])
         for side, way in ((0, 1), (1, SIDE - 1)):
             base = 4 * part * ((u + way) % SIDE)
             cut = rows(base + 2 * part * side, 2 * part)
-            p[n, cut, :] = (p[n, cut, :].astype(F32) + a1[n, side].astype(F32)).astype(BF16)
+            p[n, cut, :] = (p[n, cut, :].astype(F32) + a1_q[n, side].astype(F32)).astype(BF16)
             send(
-                p.at[n, rows(base, 4 * part), :], b1.at[n, side],
+                p.at[n, rows(base, 4 * part), :], b1_q.at[n, side],
                 sum_s.at[1, kind], b1_r.at[j], peer(j, True, way),
             )
 
     def sum1(j):
-        n, part, (p, a1, b1, tt, r2, m_), kind = layout(j)
+        n, part, (p, tt, r2, m_), kind = layout(j)
         u, v = axes(j)
-        got(b1.at[n], b1_r.at[j])
         total = p[n, rows(4 * part * u, 4 * part), :].astype(F32)
-        total = total + b1[n, 0].astype(F32) + b1[n, 1].astype(F32)
+        if kind:
+            got(r1_o.at[n], a1_r.at[j])
+            total = total + r1_o[n, 0].astype(F32) + r1_o[n, 1].astype(F32) + r1_o[n, 2].astype(F32)
+        else:
+            got(b1_q.at[n], b1_r.at[j])
+            total = total + b1_q[n, 0].astype(F32) + b1_q[n, 1].astype(F32)
         tt[n] = total.astype(BF16)
         for i in range(1, SIDE):
             to = (v + i) % SIDE
@@ -278,7 +319,7 @@
             )
 
     def sum2(j):
-        n, part, (p, a1, b1, tt, r2, m_), kind = layout(j)
+        n, part, (p, tt, r2, m_), kind = layout(j)
         u, v = axes(j)
         got(r2.at[n], r2_r.at[j])
         total = tt[n, rows(part * v, part), :].astype(F32)
@@ -293,32 +334,37 @@
             )
 
     def gather1(j):
-        n, part, (p, a1, b1, tt, r2, m_), kind = layout(j)
+        n, part, (p, tt, r2, m_), kind = layout(j)
         u, v = axes(j)
         got(r2.at[n], g1_r.at[j])
         own = rows(4 * part * u, 4 * part)
-        for way in (1, SIDE - 1):
+        for way in range(1, SIDE) if kind else (1, SIDE - 1):
             send(
                 m_.at[n, k, own, :], m_.at[n, k, own, :],
                 sum_s.at[4, kind], g2_r.at[j], peer(j, True, way),
             )
 
     def gather2(j):
-        n, part, (p, a1, b1, tt, r2, m_), kind = layout(j)
+        n, part, (p, tt, r2, m_), kind = layout(j)
         u, v = axes(j)
-        got(b1.at[n], g2_r.at[j])
+        got(b1_q.at[n], g2_r.at[j])
         for side, way in ((0, 1), (1, SIDE - 1)):
             base = 4 * part * ((u + SIDE - way) % SIDE) + 2 * part * side
             block = m_.at[n, k, rows(base, 2 * part), :]
             send(block, block, sum_s.at[5, kind], g3_r.at[j], peer(j, True, way))
 
     def gather3(j):
-        n, part, (p, a1, b1, tt, r2, m_), kind = layout(j)
-        got(a1.at[n], g3_r.at[j])
+        n, part, (p, tt, r2, m_), kind = layout(j)
+        if kind:
+            got(r1_o.at[n], g2_r.at[j])
+        else:
+            got(a1_q.at[n], g3_r.at[j])
         send(m_.at[n, k], m_.at[n, k], sum_s.at[6, kind], h_r.at[j], partner)
 
+    begun = []
+
     def joined(j):
-        n, part, (p, a1, b1, tt, r2, m_), kind = layout(j)
+        n, part, (p, tt, r2, m_), kind = layout(j)
         got(m_.at[n, 1 - k], h_r.at[j])
         if j < PIECES:
             piece = ctx[:, W * j : W * (j + 1)]
@@ -326,17 +372,17 @@
                 for side in range(2):
                     cols = slice(W * side, W * (side + 1))
                     term = mm(piece, m_[n, side, W * m : W * (m + 1), :])
-                    if j == 0:
+                    if not begun:
                         acc[m, :, cols] = term
                     else:
                         acc[m, :, cols] = acc[m, :, cols] + term
+            begun.append(j)
 
     def sums_end():
-        for kind in range(2):
-            p, a1, b1, tt, r2, m_ = layout(kind * PIECES)[2]
-            for i, ref in enumerate((a1, b1, r2, r2, b1, a1)):
-                sent(ref, sum_s.at[i, kind])
-            sent(m_.at[:, 0], sum_s.at[6, kind])
+        for i, ref in enumerate((a1_q, b1_q, r2_q, r2_q, b1_q, a1_q, m_q.at[:, 0])):
+            sent(ref, sum_s.at[i, 0])
+        for i, ref in ((0, r1_o), (2, r2_o), (3, r2_o), (4, r1_o), (6, m_o.at[:, 0])):
+            sent(ref, sum_s.at[i, 1])
 
     def pool():
         len_row, len_col, route_row, route_col, end_row, end_col, slot_row, slot_col = tables(
@@ -344,7 +390,7 @@
         )
         values = states[...].astype(F32)
         scale = lax.rsqrt(jnp.mean(values * values, axis=-1, keepdims=True) + EPS)
-        normed = values * scale * gain[...]
+        normed = values * scale * gain[...].reshape(1, -1)
         high = normed.astype(BF16)
         low = (normed - high.astype(F32)).astype(BF16)
         n = states.shape[0]
@@ -387,29 +433,29 @@
         pick = onehot(spot == base + 2 * PIECES + slot % 2)
         ctx[own, E : E + FLAGS] = mm(pick, arrived[:, :FLAGS]).astype(BF16)
 
-    def ctx_block(plane, side):
+    def ctx_cut(plane, cut):
         plane = (plane + 2 * NT) % NT
-        if side is None:
-            return ctx.at[rows(2 * NB * plane, 2 * NB), :]
-        return ctx.at[rows(2 * NB * plane + NB * side, NB), :]
-
-    def ctx_send(step):
-        cut = step == 3
+        return ctx.at[rows(2 * NB * plane + NB * cut, NB), :]
+
+    def ctx_send(step, cut):
         for side, sign, dev in ((0, -1, up), (1, 1, down)):
-            block = ctx_block(t + sign * step, side if cut else None)
-            send(block, block, c_s.at[side], c_r.at[side, step], dev)
-
-    def ctx_got(step):
-        cut = step == 3
-        for side, sign, dev in ((0, -1, up), (1, 1, down)):
-            block = ctx_block(t + sign * (step + 1), side if cut else None)
-            got(block, c_r.at[side, step])
+            if step < 3 or side == cut:
+                block = ctx_cut(t + sign * step, cut)
+                send(block, block, c_s.at[side], c_r.at[side, step, cut], dev)
+
+    def ctx_step(step, cut):
+        for side, sign in ((0, -1), (1, 1)):
+            if step < 3 or side == cut:
+                got(ctx_cut(t + sign * (step + 1), cut), c_r.at[side, step, cut])
+        if step < 3:
+            ctx_send(step + 1, cut)
 
     def ctx_end():
         for side in range(2):
             sent(ctx.at[pl.ds(0, 7 * NB), :], c_s.at[side])
 
     def latents():
+        load_wait("in")
         part = mm(ctx[:, :E], w_in[...]).astype(BF16)
         lat[...] = part
         wide = part.astype(F32)
@@ -435,22 +481,30 @@
 
     def project():
         scale = scales()
-        for m in range(3):
-            qkv[m] = (acc[m] * scale).astype(BF16)
+        for m in range(2):
+            qk[m] = (acc[m] * scale).astype(BF16)
+        values = (acc[2] * scale).astype(BF16)
+        for h in range(values.shape[1] // DH):
+            vals[:, 2 * DH * h : 2 * DH * h + DH] = values[:, DH * h : DH * (h + 1)]
+
+    def mask():
+        for h in range(vals.shape[1] // (2 * DH)):
+            vals[:, 2 * DH * h + DH : 2 * DH * (h + 1)] = jnp.ones((CTX, DH), BF16)
+        seen = mm_t(jnp.ones((8, FLAGS), BF16), ctx[:, E : E + FLAGS])[0:1, :] > 0.5
+        line, place = iota((CTX, CTX), 0), iota((CTX, CTX), 1)
+        allowed = ((place < line) & seen) | (place == line)
+        bias[...] = jnp.where(allowed, 0.0, -1e30)
 
     def head(h):
         cols = slice(DH * h, DH * (h + 1))
-        seen = mm_t(jnp.ones((8, FLAGS), BF16), ctx[:, E : E + FLAGS])[0:1, :] > 0.5
         for i in range(CTX // 128):
             lines = slice(128 * i, 128 * (i + 1))
             n = 128 * (i + 1)
-            scores = mm_t(qkv[0, lines, cols], qkv[1, :n, cols]) * DH ** (-0.5)
-            line, place = iota((128, n), 0) + 128 * i, iota((128, n), 1)
-            allowed = ((place < line) & seen[:, :n]) | (place == line)
-            scores = jnp.where(allowed, scores, -1e30)
-            raised = jnp.exp(scores - jnp.max(scores, axis=-1, keepdims=True))
-            weights = raised / jnp.sum(raised, axis=-1, keepdims=True)
-            att[lines, cols] = mm(weights.astype(BF16), qkv[2, :n, cols]).astype(BF16)
+            scores = mm_t(qk[0, lines, cols], qk[1, :n, cols])
+            scores = scores * (DH ** (-0.5) * LOG2E) + bias[lines, :n]
+            raised = jnp.exp2(scores - jnp.max(scores, axis=-1, keepdims=True)).astype(BF16)
+            mixed = mm(raised, vals[:n, 2 * DH * h : 2 * DH * (h + 1)])
+            att[lines, cols] = (mixed[:, :DH] / mixed[:, DH:]).astype(BF16)
 
     def z_rows(plane, start, size):
         plane = (plane + 2 * NT) % NT
@@ -482,6 +536,8 @@
                 z_s.at[1], z_r.at[n, step], dev,
             )
 
+    packed = []
+
     def z_last(n):
         got(zr.at[n, 3], z_r.at[n, 3])
         total = zp[n, z_rows(t, 0, 2 * NB), :].astype(F32)
@@ -489,10 +545,8 @@
         spot, slot = iota((NB * PACK, 2 * NB), 0), iota((NB * PACK, 2 * NB), 1)
         pick = onehot(spot == (slot // 2) * PACK + (slot % 2) * PIECES + n)
         term = mm(pick, total.astype(BF16))
-        if n == 0:
-            packf[...] = term
-        else:
-            packf[...] = packf[...] + term
+        packf[...] = packf[...] + term if packed else term
+        packed.append(n)
 
     def z_end():
         sent(zr.at[:, 0, :, pl.ds(0, NB), :], z_s.at[0])
@@ -502,31 +556,35 @@
         len_row, len_col, route_row, route_col, end_row, end_col, slot_row, slot_col = tables(
             lengths, route
         )
-        n = states.shape[0]
-        place = iota((n, lengths.shape[1]), 0).astype(F32)
+        n, patches = states.shape[0], lengths.shape[1]
+        place = iota((n, patches), 0).astype(F32)
         member = onehot((place >= end_row - len_row) & (place < end_row))
-        spot = iota((lengths.shape[1], NB * PACK), 1).astype(F32)
+        spot = iota((patches, NB * PACK), 1).astype(F32)
         target = route_col * PACK + slot_col * PIECES
-        total = jnp.zeros((n, w_head.shape[1]), F32)
+        picks = jnp.concatenate([onehot(spot == target + j) for j in range(PIECES)], axis=0)
+        values = mm(picks, arr2[...]).astype(BF16)
+        total = jnp.zeros((patches, w_head.shape[1]), F32)
         for j in range(PIECES):
-            cols = slice(W * j, W * (j + 1))
-            values = mm(onehot(spot == target + j), arr2[...]).astype(BF16)
-            decoded = (states[:, cols].astype(F32) + mm(member, values)).astype(BF16)
-            total = total + mm(decoded, w_head[cols, :])
-        out[...] = total.astype(BF16)
+            total = total + mm(values[patches * j : patches * (j + 1), :], w_head[W * j : W * (j + 1), :])
+        high = total.astype(BF16)
+        low = (total - high.astype(F32)).astype(BF16)
+        out[...] = (base[...] + mm(member, high) + mm(member, low)).astype(BF16)
+
+    def own_logits():
+        load_wait("head")
+        base[...] = mm(states[...], w_head[...])
 
     def add_residual():
+        load_wait("out")
         lw[...] = mm(lat[...], w_out[...])
 
     def exch():
         exchange_wait(snd, arr, a_s, a_r)
         slots()
-        ctx_send(0)
-
-    def ctx_step(step):
-        ctx_got(step)
-        if step < 3:
-            ctx_send(step + 1)
+
+    def ctx_go():
+        ctx_send(0, 0)
+        ctx_send(0, 1)
 
     def finish():
         sent(wsc.at[:, :, theirs], x_s.at[0])
@@ -539,12 +597,15 @@
     stages = {
         "start": start, "relay": relay, "product": product, "turn": turn, "sum1": sum1,
         "sum2": sum2, "gather1": gather1, "gather2": gather2, "gather3": gather3,
-        "joined": joined, "exch": exch, "ctx": ctx_step, "lat": latents, "res": add_residual,
+        "joined": joined, "exch": exch, "ctxgo": ctx_go, "ctx": ctx_step, "lat": latents, "res": add_residual, "mask": mask, "own": own_logits,
         "proj": project, "head": head, "zf": z_first, "za": z_add, "zl": z_last,
     }
+    load_start()
     greet()
+    load_wait("gain", "scale", "lengths", "route", "states")
+    pool()
+    load_wait("q", "k", "v", "ao")
     scale_weights()
-    pool()
     meet()
     swap_weights()
     start(0)
@@ -564,13 +625,20 @@
     w_query, w_key, w_value, w_attn_out, w_out, w_head,
 ):
     vmem = pl.BlockSpec(memory_space=pltpu.VMEM)
+    far = pl.BlockSpec(memory_space=pl.ANY)
     dma = pltpu.SemaphoreType.DMA
     part_q, part_o = 3 * W // 16, W // 16
 
     def buf(*shape, dtype=BF16):
         return pltpu.VMEM(shape, dtype)
 
+    inputs = (
+        byte_states, enc_gain, patch_lengths, patch_route.reshape(1, -1), w_in,
+        latent_gain.reshape(NB, -1), w_query, w_key, w_value, w_attn_out, w_out, w_head,
+    )
     scratch = [
+        *[buf(*value.shape, dtype=value.dtype) for value in inputs],
+        dma((len(inputs),)),
         buf(STAGES, W, W),
         buf(3, 128, 2 * W),
         buf(3, W, W),
@@ -578,9 +646,8 @@
         buf(PIECES, 3 * W, W),
         buf(PIECES, W, W),
         buf(PIECES, 2, 2 * part_q, W),
-        buf(PIECES, 2, 2 * part_o, W),
         buf(PIECES, 2, 4 * part_q, W),
-        buf(PIECES, 2, 4 * part_o, W),
+        buf(PIECES, 3, 4 * part_o, W),
         buf(PIECES, 4 * part_q, W),
         buf(PIECES, 4 * part_o, W),
         buf(PIECES, 3, part_q, W),
@@ -595,31 +662,33 @@
         buf(CTX, 2 * W),
         buf(NT, 8, CTX, dtype=F32),
         buf(3, CTX, 2 * W, dtype=F32),
-        buf(3, CTX, 2 * W),
+        buf(2, CTX, 2 * W),
+        buf(CTX, 4 * W),
+        buf(CTX, CTX, dtype=F32),
+        buf(byte_states.shape[0], w_head.shape[1], dtype=F32),
         buf(CTX, 2 * W),
         buf(CTX, E, dtype=F32),
         buf(PIECES, CTX, W),
         buf(PIECES, 4, 2, 2 * NB, W),
         buf(NB * PACK, W, dtype=F32),
-        dma((2,)), dma((STAGES,)), dma, dma((STAGES,)), dma((STAGES,)),
-        dma((2,)), dma((2,)), dma, dma, dma((2,)), dma((2, 4)), dma, dma,
+        dma((2,)), dma((STAGES, 2)), dma, dma((STAGES,)), dma((STAGES,)),
+        dma((2,)), dma((2,)), dma, dma, dma((2,)), dma((2, 4, 2)), dma, dma,
         dma((7, 2)),
-        dma((STAGES,)), dma((STAGES,)), dma((STAGES,)), dma((STAGES,)), dma((STAGES,)),
-        dma((STAGES,)), dma((STAGES,)),
+        dma((STAGES,)), dma((PIECES,)), dma((STAGES,)), dma((STAGES,)), dma((STAGES,)),
+        dma((PIECES,)), dma((STAGES,)),
         dma((2,)), dma((PIECES, 4)), dma, dma,
     ]
     return pl.pallas_call(
         kernel,
         out_shape=jax.ShapeDtypeStruct((byte_states.shape[0], w_head.shape[1]), BF16),
-        in_specs=[vmem] * 12,
+        in_specs=[far] * 12,
         out_specs=vmem,
         scratch_shapes=scratch,
         compiler_params=pltpu.CompilerParams(
             collective_id=0, has_side_effects=True, vmem_limit_bytes=56 * 1024 * 1024
         ),
     )(
-        byte_states, enc_gain.reshape(1, -1), patch_lengths, patch_route.reshape(1, -1), w_in,
-        latent_gain.reshape(NB, -1), w_query, w_key, w_value, w_attn_out, w_out, w_head,
+        *inputs
     )
 
 

time: 112 us -> 96.1 us (0.86)
  Pallas kernels: 109 us -> 94.3 us
  local copies, waits for them, and re-layouts: 2.86 us -> 1.57 us
    pallas_call x1, Pallas kernels: 109 us -> 94.3 us  [body(): pl.pallas_call(kernel, out_shape=jax.ShapeDtypeStruct((byte_states.shape[...]
    reshape x1 -> x0, local copies, waits for them, and re-layouts: 1.29 us -> none  [body(): enc_gain.reshape(1, -1)]
where the time goes in v4:
time: 96.1 us; the launch traced here: 95.9 us
  Pallas kernels  94.3 us (98%)
  local copies, waits for them, and re-layouts  1.57 us (2%)
    pallas_call x1, Pallas kernels, body(): pl.pallas_call(kernel, out_shape=jax.ShapeDtypeStruct((byte_states.shape[...  94.3 us

profile of v4, /device:TPU:1, one launch (start us, length us, event | category | flops | bytes accessed | tf_op | source)
XLA Modules:
  0.0 95.9 jit_solution(13414656610987738896)
XLA Ops:
  0.0 94.3 %shard_map.118 = bf16[256,256]{1,0:T(8,128)(2,1)} custom-call(bf16[256,1280]{1,0:T(8,128)(2,1)} %states_far.1, f32[1280]{0:T(1024)} %gain_far.1, s32[1,32]{1,0:T(1,128)} %lengths_far.1, s32[1,32]{1,0:T(1,128)} %bitcast.3, bf16[1280,512]{1,0:T(8,128)(2,1)} %w_in_far.1, f32[32,128]{1,0:T(8,128)} %bitcast.2, bf16[128,512]{1,0:T(8,128)(2,1)} %w_q_far.1, ...), custom_call_target="tpu_custom_call" | custom-call | tf_op jit(solution)/shard_map/pallas_call | solution.py:681
  94.3 1.6 %copy.14 = bf16[256,256]{1,0:T(8,128)(2,1)} copy(bf16[256,256]{1,0:T(8,128)(2,1)} %shard_map.118) | data formatting | bytes 262144

commit v5 on v4

--- a/solution.py
+++ b/solution.py
@@ -23,34 +23,34 @@
 FLAGS = 128
 PACK = 16
 
+(
+    START, RELAY, PRODUCT, TURN, SUM1, SUM2, GATHER1, GATHER2, GATHER3, JOINED, EXCH,
+    CTXGO, RING, LAT, RES, MASK, OWN, PROJ, HEAD, ZF, ZA, ZL,
+) = range(22)
 ORDER = (
-    ("start", 2), ("start", 3), ("start", 4), ("relay", 0, 1), ("relay", 1, 1), ("relay", 0, 2),
-    ("relay", 2, 1), ("relay", 1, 2), ("relay", 3, 1), ("exch",), ("relay", 0, 3), ("start", 5),
-    ("relay", 2, 2), ("relay", 4, 1), ("relay", 1, 3), ("start", 6), ("relay", 3, 2),
-    ("relay", 0, 4), ("relay", 5, 1), ("relay", 2, 3), ("start", 7), ("relay", 4, 2),
-    ("product", 0), ("relay", 1, 4), ("relay", 6, 1), ("relay", 3, 3), ("start", 8), ("product", 1),
-    ("relay", 5, 2), ("relay", 2, 4), ("relay", 7, 1), ("relay", 4, 3), ("product", 2),
-    ("start", 9), ("relay", 6, 2), ("relay", 3, 4), ("turn", 0), ("relay", 8, 1), ("relay", 5, 3),
-    ("product", 3), ("relay", 7, 2), ("relay", 4, 4), ("turn", 1), ("relay", 9, 1), ("relay", 6, 3),
-    ("product", 4), ("relay", 8, 2), ("turn", 2), ("relay", 5, 4), ("relay", 7, 3), ("relay", 9, 2),
-    ("turn", 3), ("relay", 6, 4), ("product", 5), ("sum1", 0), ("relay", 8, 3), ("turn", 4),
-    ("relay", 7, 4), ("product", 6), ("sum1", 1), ("relay", 9, 3), ("ctxgo",), ("relay", 8, 4),
-    ("product", 7), ("sum1", 2), ("sum1", 3), ("relay", 9, 4), ("product", 8), ("sum1", 5),
-    ("ctx", 0, 0), ("sum1", 4), ("product", 9), ("sum2", 0), ("sum1", 6), ("ctx", 0, 1),
-    ("sum1", 7), ("sum2", 1), ("own",), ("sum2", 2), ("sum2", 3), ("ctx", 1, 0), ("sum2", 4),
-    ("sum1", 8), ("sum2", 5), ("sum2", 7), ("ctx", 1, 1), ("sum1", 9), ("gather1", 1),
-    ("gather1", 0), ("sum2", 6), ("gather1", 3), ("gather1", 5), ("ctx", 2, 0), ("gather1", 2),
-    ("gather1", 7), ("gather1", 4), ("sum2", 8), ("sum2", 9), ("ctx", 2, 1), ("ctx", 3, 0),
-    ("gather2", 1), ("gather2", 0), ("gather1", 6), ("ctx", 3, 1), ("gather2", 2), ("gather2", 3),
-    ("lat",), ("mask",), ("gather3", 5), ("gather2", 4), ("gather1", 9), ("gather3", 7),
-    ("gather1", 8), ("gather3", 0), ("joined", 5), ("joined", 7), ("gather3", 1), ("res",),
-    ("gather3", 6), ("gather3", 3), ("joined", 0), ("gather3", 2), ("joined", 1), ("gather3", 9),
-    ("gather3", 4), ("joined", 6), ("joined", 3), ("gather3", 8), ("joined", 2), ("joined", 9),
-    ("joined", 4), ("joined", 8), ("proj",), ("head", 0), ("head", 1), ("head", 2), ("head", 3),
-    ("zf", 0), ("zf", 1), ("zf", 2), ("zf", 3), ("zf", 4), ("za", 0, 1), ("za", 1, 1), ("za", 2, 1),
-    ("za", 3, 1), ("za", 4, 1), ("za", 0, 2), ("za", 1, 2), ("za", 2, 2), ("za", 3, 2),
-    ("za", 4, 2), ("za", 0, 3), ("za", 1, 3), ("za", 2, 3), ("za", 3, 3), ("za", 4, 3), ("zl", 0),
-    ("zl", 1), ("zl", 2), ("zl", 3), ("zl", 4),
+    (START, 2), (START, 3), (START, 4), (RELAY, 0, 1), (RELAY, 1, 1), (RELAY, 0, 2), (RELAY, 2, 1),
+    (RELAY, 1, 2), (EXCH,), (RELAY, 3, 1), (RELAY, 0, 3), (START, 5), (RELAY, 2, 2), (RELAY, 4, 1),
+    (RELAY, 1, 3), (START, 6), (RELAY, 3, 2), (RELAY, 0, 4), (RELAY, 5, 1), (RELAY, 2, 3),
+    (START, 7), (RELAY, 4, 2), (PRODUCT, 0), (RELAY, 1, 4), (RELAY, 6, 1), (RELAY, 3, 3),
+    (START, 8), (PRODUCT, 1), (RELAY, 5, 2), (RELAY, 2, 4), (RELAY, 7, 1), (RELAY, 4, 3),
+    (PRODUCT, 2), (START, 9), (RELAY, 6, 2), (RELAY, 3, 4), (TURN, 0), (RELAY, 8, 1), (RELAY, 5, 3),
+    (PRODUCT, 3), (RELAY, 7, 2), (RELAY, 4, 4), (TURN, 1), (RELAY, 9, 1), (RELAY, 6, 3),
+    (PRODUCT, 4), (RELAY, 8, 2), (TURN, 2), (RELAY, 5, 4), (RELAY, 7, 3), (RELAY, 9, 2), (TURN, 3),
+    (RELAY, 6, 4), (PRODUCT, 5), (SUM1, 0), (RELAY, 8, 3), (TURN, 4), (RELAY, 7, 4), (PRODUCT, 6),
+    (SUM1, 1), (RELAY, 9, 3), (CTXGO,), (RELAY, 8, 4), (PRODUCT, 7), (SUM1, 2), (SUM1, 3),
+    (RELAY, 9, 4), (PRODUCT, 8), (SUM1, 5), (RING, 0, 0), (SUM1, 4), (PRODUCT, 9), (SUM2, 0),
+    (SUM1, 6), (RING, 0, 1), (SUM1, 7), (SUM2, 1), (OWN,), (SUM2, 2), (SUM2, 3), (RING, 1, 0),
+    (SUM2, 4), (SUM1, 8), (SUM2, 5), (SUM2, 7), (RING, 1, 1), (SUM1, 9), (GATHER1, 1), (GATHER1, 0),
+    (SUM2, 6), (GATHER1, 3), (GATHER1, 5), (RING, 2, 0), (GATHER1, 2), (GATHER1, 7), (GATHER1, 4),
+    (SUM2, 8), (SUM2, 9), (RING, 2, 1), (RING, 3, 0), (GATHER2, 1), (GATHER2, 0), (GATHER1, 6),
+    (RING, 3, 1), (GATHER2, 2), (GATHER2, 3), (LAT,), (MASK,), (GATHER3, 5), (GATHER2, 4),
+    (GATHER1, 9), (GATHER3, 7), (GATHER1, 8), (GATHER3, 0), (JOINED, 5), (JOINED, 7), (GATHER3, 1),
+    (RES,), (GATHER3, 6), (GATHER3, 3), (JOINED, 0), (GATHER3, 2), (JOINED, 1), (GATHER3, 9),
+    (GATHER3, 4), (JOINED, 6), (JOINED, 3), (GATHER3, 8), (JOINED, 2), (JOINED, 9), (JOINED, 4),
+    (JOINED, 8), (PROJ,), (HEAD, 0), (ZF, 0), (ZF, 1), (ZF, 2), (ZF, 3), (ZF, 4), (HEAD, 1),
+    (ZA, 0, 1), (ZA, 1, 1), (ZA, 2, 1), (ZA, 3, 1), (ZA, 4, 1), (HEAD, 2), (ZA, 0, 2), (ZA, 1, 2),
+    (ZA, 2, 2), (ZA, 3, 2), (ZA, 4, 2), (HEAD, 3), (ZA, 0, 3), (ZA, 1, 3), (ZA, 2, 3), (ZA, 3, 3),
+    (ZA, 4, 3), (HEAD, 4), (ZL, 0), (ZL, 1), (ZL, 2), (ZL, 3), (ZL, 4),
 )
 
 
@@ -495,24 +495,36 @@
         allowed = ((place < line) & seen) | (place == line)
         bias[...] = jnp.where(allowed, 0.0, -1e30)
 
-    def head(h):
-        cols = slice(DH * h, DH * (h + 1))
-        for i in range(CTX // 128):
-            lines = slice(128 * i, 128 * (i + 1))
-            n = 128 * (i + 1)
-            scores = mm_t(qk[0, lines, cols], qk[1, :n, cols])
-            scores = scores * (DH ** (-0.5) * LOG2E) + bias[lines, :n]
+    def planes(step):
+        return (t + 4,) if step == 0 else (t,) if step == 4 else (t + 4 - step, t - 4 + step)
+
+    def head(step):
+        lines = [z_rows(plane, 0, 2 * NB) for plane in planes(step)]
+        size = 2 * NB * len(lines)
+        asks = jnp.concatenate([qk[0, line, :] for line in lines], axis=0)
+        hide = jnp.concatenate([bias[line, :] for line in lines], axis=0)
+        for h in range(asks.shape[1] // DH):
+            cols = slice(DH * h, DH * (h + 1))
+            scores = mm_t(asks[:, cols], qk[1, :, cols]) * (DH ** (-0.5) * LOG2E) + hide
             raised = jnp.exp2(scores - jnp.max(scores, axis=-1, keepdims=True)).astype(BF16)
-            mixed = mm(raised, vals[:n, 2 * DH * h : 2 * DH * (h + 1)])
-            att[lines, cols] = (mixed[:, :DH] / mixed[:, DH:]).astype(BF16)
+            mixed = mm(raised, vals[:, 2 * DH * h : 2 * DH * (h + 1)])
+            att[0:size, cols] = (mixed[:, :DH] / mixed[:, DH:]).astype(BF16)
+
+    def outputs(n, step):
+        lines = [z_rows(plane, 0, 2 * NB) for plane in planes(step)]
+        size = 2 * NB * len(lines)
+        value = mm(att[0:size, :W], m_o[n, 0]) + mm(att[0:size, W:], m_o[n, 1])
+        cols = slice(W * n, W * (n + 1))
+        return [
+            value[2 * NB * i : 2 * NB * (i + 1), :] + lw[line, cols] for i, line in enumerate(lines)
+        ]
 
     def z_rows(plane, start, size):
         plane = (plane + 2 * NT) % NT
         return rows(2 * NB * plane + start, size)
 
     def z_first(n):
-        value = mm(att[:, :W], m_o[n, 0]) + mm(att[:, W:], m_o[n, 1])
-        zp[n] = (value + lw[:, W * n : W * (n + 1)]).astype(BF16)
+        zp[n, z_rows(t + 4, 0, 2 * NB), :] = outputs(n, 0)[0].astype(BF16)
         for side, dev in ((0, up), (1, down)):
             send(
                 zp.at[n, z_rows(t + 4, NB * side, NB), :], zr.at[n, 0, side, pl.ds(0, NB), :],
@@ -520,27 +532,29 @@
             )
 
     def z_add(n, step):
+        values = outputs(n, step)
         if step == 1:
             got(zr.at[n, 0, :, pl.ds(0, NB), :], z_r.at[n, 0])
         else:
             got(zr.at[n, step - 1], z_r.at[n, step - 1])
         for side, sign, dev in ((0, 1, up), (1, -1, down)):
-            plane = t + sign * (4 - step)
+            value = values[side]
+            place = z_rows(t + sign * (4 - step), 0, 2 * NB)
             if step == 1:
-                place, came = z_rows(plane, NB * side, NB), zr[n, 0, side, 0:NB, :]
+                came = zr[n, 0, side, 0:NB, :].astype(F32)
+                whole = [value[:NB, :], value[NB:, :]]
+                whole[side] = whole[side] + came
+                value = jnp.concatenate(whole, axis=0)
             else:
-                place, came = z_rows(plane, 0, 2 * NB), zr[n, step - 1, side]
-            zp[n, place, :] = (zp[n, place, :].astype(F32) + came.astype(F32)).astype(BF16)
-            send(
-                zp.at[n, z_rows(plane, 0, 2 * NB), :], zr.at[n, step, side],
-                z_s.at[1], z_r.at[n, step], dev,
-            )
+                value = value + zr[n, step - 1, side].astype(F32)
+            zp[n, place, :] = value.astype(BF16)
+            send(zp.at[n, place, :], zr.at[n, step, side], z_s.at[1], z_r.at[n, step], dev)
 
     packed = []
 
     def z_last(n):
+        total = outputs(n, 4)[0]
         got(zr.at[n, 3], z_r.at[n, 3])
-        total = zp[n, z_rows(t, 0, 2 * NB), :].astype(F32)
         total = total + zr[n, 3, 0].astype(F32) + zr[n, 3, 1].astype(F32)
         spot, slot = iota((NB * PACK, 2 * NB), 0), iota((NB * PACK, 2 * NB), 1)
         pick = onehot(spot == (slot // 2) * PACK + (slot % 2) * PIECES + n)
@@ -595,10 +609,11 @@
         z_end()
 
     stages = {
-        "start": start, "relay": relay, "product": product, "turn": turn, "sum1": sum1,
-        "sum2": sum2, "gather1": gather1, "gather2": gather2, "gather3": gather3,
-        "joined": joined, "exch": exch, "ctxgo": ctx_go, "ctx": ctx_step, "lat": latents, "res": add_residual, "mask": mask, "own": own_logits,
-        "proj": project, "head": head, "zf": z_first, "za": z_add, "zl": z_last,
+        START: start, RELAY: relay, PRODUCT: product, TURN: turn, SUM1: sum1,
+        SUM2: sum2, GATHER1: gather1, GATHER2: gather2, GATHER3: gather3,
+        JOINED: joined, EXCH: exch, CTXGO: ctx_go, RING: ctx_step, LAT: latents,
+        RES: add_residual, MASK: mask, OWN: own_logits,
+        PROJ: project, HEAD: head, ZF: z_first, ZA: z_add, ZL: z_last,
     }
     load_start()
     greet()
@@ -666,7 +681,7 @@
         buf(CTX, 4 * W),
         buf(CTX, CTX, dtype=F32),
         buf(byte_states.shape[0], w_head.shape[1], dtype=F32),
-        buf(CTX, 2 * W),
+        buf(4 * NB, 2 * W),
         buf(CTX, E, dtype=F32),
         buf(PIECES, CTX, W),
         buf(PIECES, 4, 2, 2 * NB, W),

time: 96.1 us -> 93.9 us (0.977)
  Pallas kernels: 94.3 us -> 92.2 us
    pallas_call x1, Pallas kernels: 94.3 us -> 92.2 us  [body(): pl.pallas_call(kernel, out_shape=jax.ShapeDtypeStruct((byte_states.shape[...]
where the time goes in v5:
time: 93.9 us; the launch traced here: 93.8 us
  Pallas kernels  92.2 us (98%)
  local copies, waits for them, and re-layouts  1.57 us (2%)
    pallas_call x1, Pallas kernels, body(): pl.pallas_call(kernel, out_shape=jax.ShapeDtypeStruct((byte_states.shape[...  92.2 us

profile of v5, /device:TPU:1, one launch (start us, length us, event | category | flops | bytes accessed | tf_op | source)
XLA Modules:
  0.0 93.8 jit_solution(16232876907531143824)
XLA Ops:
  0.0 92.2 %shard_map.118 = bf16[256,256]{1,0:T(8,128)(2,1)} custom-call(bf16[256,1280]{1,0:T(8,128)(2,1)} %states_far.1, f32[1280]{0:T(1024)} %gain_far.1, s32[1,32]{1,0:T(1,128)} %lengths_far.1, s32[1,32]{1,0:T(1,128)} %bitcast.3, bf16[1280,512]{1,0:T(8,128)(2,1)} %w_in_far.1, f32[32,128]{1,0:T(8,128)} %bitcast.2, bf16[128,512]{1,0:T(8,128)(2,1)} %w_q_far.1, ...), custom_call_target="tpu_custom_call" | custom-call | tf_op jit(solution)/shard_map/pallas_call | solution.py:696
  92.2 1.6 %copy.14 = bf16[256,256]{1,0:T(8,128)(2,1)} copy(bf16[256,256]{1,0:T(8,128)(2,1)} %shard_map.118) | data formatting | bytes 262144

commit v6 on v5

--- a/solution.py
+++ b/solution.py
@@ -10,6 +10,8 @@
 F32 = jnp.float32
 DH = 128
 EPS = 1e-06
+LANES = 128
+EARLY, LATE = 8, 2
 LOG2E = 1.4426950408889634
 SIDE = 4
 NB = 32
@@ -25,8 +27,8 @@
 
 (
     START, RELAY, PRODUCT, TURN, SUM1, SUM2, GATHER1, GATHER2, GATHER3, JOINED, EXCH,
-    CTXGO, RING, LAT, RES, MASK, OWN, PROJ, HEAD, ZF, ZA, ZL,
-) = range(22)
+    CTXGO, RING, LAT, MASK, OWN, PROJ, HEAD, ZF, ZA, ZL,
+) = range(21)
 ORDER = (
     (START, 2), (START, 3), (START, 4), (RELAY, 0, 1), (RELAY, 1, 1), (RELAY, 0, 2), (RELAY, 2, 1),
     (RELAY, 1, 2), (EXCH,), (RELAY, 3, 1), (RELAY, 0, 3), (START, 5), (RELAY, 2, 2), (RELAY, 4, 1),
@@ -35,22 +37,22 @@
     (START, 8), (PRODUCT, 1), (RELAY, 5, 2), (RELAY, 2, 4), (RELAY, 7, 1), (RELAY, 4, 3),
     (PRODUCT, 2), (START, 9), (RELAY, 6, 2), (RELAY, 3, 4), (TURN, 0), (RELAY, 8, 1), (RELAY, 5, 3),
     (PRODUCT, 3), (RELAY, 7, 2), (RELAY, 4, 4), (TURN, 1), (RELAY, 9, 1), (RELAY, 6, 3),
-    (PRODUCT, 4), (RELAY, 8, 2), (TURN, 2), (RELAY, 5, 4), (RELAY, 7, 3), (RELAY, 9, 2), (TURN, 3),
-    (RELAY, 6, 4), (PRODUCT, 5), (SUM1, 0), (RELAY, 8, 3), (TURN, 4), (RELAY, 7, 4), (PRODUCT, 6),
+    (PRODUCT, 4), (RELAY, 8, 2), (RELAY, 5, 4), (TURN, 2), (RELAY, 7, 3), (RELAY, 9, 2), (TURN, 3),
+    (RELAY, 6, 4), (PRODUCT, 5), (SUM1, 0), (RELAY, 8, 3), (RELAY, 7, 4), (TURN, 4), (PRODUCT, 6),
     (SUM1, 1), (RELAY, 9, 3), (CTXGO,), (RELAY, 8, 4), (PRODUCT, 7), (SUM1, 2), (SUM1, 3),
     (RELAY, 9, 4), (PRODUCT, 8), (SUM1, 5), (RING, 0, 0), (SUM1, 4), (PRODUCT, 9), (SUM2, 0),
-    (SUM1, 6), (RING, 0, 1), (SUM1, 7), (SUM2, 1), (OWN,), (SUM2, 2), (SUM2, 3), (RING, 1, 0),
-    (SUM2, 4), (SUM1, 8), (SUM2, 5), (SUM2, 7), (RING, 1, 1), (SUM1, 9), (GATHER1, 1), (GATHER1, 0),
-    (SUM2, 6), (GATHER1, 3), (GATHER1, 5), (RING, 2, 0), (GATHER1, 2), (GATHER1, 7), (GATHER1, 4),
-    (SUM2, 8), (SUM2, 9), (RING, 2, 1), (RING, 3, 0), (GATHER2, 1), (GATHER2, 0), (GATHER1, 6),
-    (RING, 3, 1), (GATHER2, 2), (GATHER2, 3), (LAT,), (MASK,), (GATHER3, 5), (GATHER2, 4),
-    (GATHER1, 9), (GATHER3, 7), (GATHER1, 8), (GATHER3, 0), (JOINED, 5), (JOINED, 7), (GATHER3, 1),
-    (RES,), (GATHER3, 6), (GATHER3, 3), (JOINED, 0), (GATHER3, 2), (JOINED, 1), (GATHER3, 9),
-    (GATHER3, 4), (JOINED, 6), (JOINED, 3), (GATHER3, 8), (JOINED, 2), (JOINED, 9), (JOINED, 4),
-    (JOINED, 8), (PROJ,), (HEAD, 0), (ZF, 0), (ZF, 1), (ZF, 2), (ZF, 3), (ZF, 4), (HEAD, 1),
-    (ZA, 0, 1), (ZA, 1, 1), (ZA, 2, 1), (ZA, 3, 1), (ZA, 4, 1), (HEAD, 2), (ZA, 0, 2), (ZA, 1, 2),
-    (ZA, 2, 2), (ZA, 3, 2), (ZA, 4, 2), (HEAD, 3), (ZA, 0, 3), (ZA, 1, 3), (ZA, 2, 3), (ZA, 3, 3),
-    (ZA, 4, 3), (HEAD, 4), (ZL, 0), (ZL, 1), (ZL, 2), (ZL, 3), (ZL, 4),
+    (SUM1, 6), (RING, 0, 1), (SUM1, 7), (SUM2, 1), (SUM2, 2), (SUM2, 3), (RING, 1, 0), (SUM2, 4),
+    (SUM1, 8), (SUM2, 5), (SUM2, 7), (RING, 1, 1), (SUM1, 9), (GATHER1, 1), (GATHER1, 0), (SUM2, 6),
+    (GATHER1, 3), (GATHER1, 2), (GATHER1, 5), (RING, 2, 0), (GATHER1, 7), (GATHER1, 4), (SUM2, 8),
+    (SUM2, 9), (RING, 2, 1), (GATHER2, 1), (RING, 3, 0), (GATHER2, 0), (GATHER1, 6), (RING, 3, 1),
+    (GATHER2, 2), (GATHER2, 3), (MASK,), (LAT,), (GATHER3, 5), (GATHER2, 4), (GATHER1, 9),
+    (GATHER3, 7), (GATHER3, 0), (GATHER1, 8), (GATHER3, 1), (JOINED, 5), (JOINED, 7), (GATHER3, 3),
+    (GATHER3, 6), (JOINED, 0), (GATHER3, 2), (JOINED, 1), (GATHER3, 4), (GATHER3, 9), (JOINED, 3),
+    (JOINED, 6), (JOINED, 2), (GATHER3, 8), (JOINED, 4), (JOINED, 9), (PROJ,), (HEAD, 0),
+    (JOINED, 8), (ZF, 0), (ZF, 1), (ZF, 2), (ZF, 3), (ZF, 4), (HEAD, 1), (OWN,), (ZA, 0, 1),
+    (ZA, 1, 1), (ZA, 2, 1), (ZA, 3, 1), (ZA, 4, 1), (HEAD, 2), (ZA, 0, 2), (ZA, 1, 2), (ZA, 2, 2),
+    (ZA, 3, 2), (ZA, 4, 2), (HEAD, 3), (ZA, 0, 3), (ZA, 1, 3), (ZA, 2, 3), (ZA, 3, 3), (ZA, 4, 3),
+    (HEAD, 4), (ZL, 0), (ZL, 1), (ZL, 2), (ZL, 3), (ZL, 4),
 )
 
 
@@ -94,7 +96,7 @@
     w_q_far, w_k_far, w_v_far, w_ao_far, w_out_far, w_head_far, out,
     states, gain, lengths, route, w_in, lat_gain, w_q, w_k, w_v, w_ao, w_out, w_head, in_s,
     blk, wsc, wx, wxo, p_q, p_o, a1_q, b1_q, r1_o, t_q, t_o, r2_q, r2_o, m_q, m_o,
-    snd, arr, snd2, arr2, ctx, lat, sqs, acc, qk, vals, bias, base, att, lw, zp, zr, packf,
+    snd, arr, snd2, arr2, ctx, lat, sqs, acc, qk, vals, bias, base, att, zp, zr, packf,
     w_s, w_r, p_s, p_r, loc, x_s, x_r, a_s, a_r, c_s, c_r, q_s, q_r,
     sum_s, a1_r, b1_r, r2_r, g1_r, g2_r, g3_r, h_r, z_s, z_r, b_s, b_r,
 ):
@@ -455,7 +457,7 @@
             sent(ctx.at[pl.ds(0, 7 * NB), :], c_s.at[side])
 
     def latents():
-        load_wait("in")
+        load_wait("in", "out")
         part = mm(ctx[:, :E], w_in[...]).astype(BF16)
         lat[...] = part
         wide = part.astype(F32)
@@ -515,9 +517,8 @@
         size = 2 * NB * len(lines)
         value = mm(att[0:size, :W], m_o[n, 0]) + mm(att[0:size, W:], m_o[n, 1])
         cols = slice(W * n, W * (n + 1))
-        return [
-            value[2 * NB * i : 2 * NB * (i + 1), :] + lw[line, cols] for i, line in enumerate(lines)
-        ]
+        value = value + mm(jnp.concatenate([lat[line, :] for line in lines], axis=0), w_out[:, cols])
+        return [value[2 * NB * i : 2 * NB * (i + 1), :] for i in range(len(lines))]
 
     def z_rows(plane, start, size):
         plane = (plane + 2 * NT) % NT
@@ -556,11 +557,21 @@
         total = outputs(n, 4)[0]
         got(zr.at[n, 3], z_r.at[n, 3])
         total = total + zr[n, 3, 0].astype(F32) + zr[n, 3, 1].astype(F32)
+        value = total.astype(BF16)
         spot, slot = iota((NB * PACK, 2 * NB), 0), iota((NB * PACK, 2 * NB), 1)
-        pick = onehot(spot == (slot // 2) * PACK + (slot % 2) * PIECES + n)
-        term = mm(pick, total.astype(BF16))
+        early = n < PIECES - 1
+        base_row = (slot // 2) * PACK + (slot % 2) * (EARLY if early else LATE) + (2 * n if early else 0)
+        term = mm(onehot(spot == base_row), value[:, :LANES])
+        term = term + mm(onehot(spot == base_row + 1), value[:, LANES:])
+        if not early:
+            snd2[1] = term.astype(BF16)
+            exchange_start(snd2.at[1], arr2.at[1], b_s.at[1], b_r.at[1])
+            return
         packf[...] = packf[...] + term if packed else term
         packed.append(n)
+        if len(packed) == PIECES - 1:
+            snd2[0] = packf[...].astype(BF16)
+            exchange_start(snd2.at[0], arr2.at[0], b_s.at[0], b_r.at[0])
 
     def z_end():
         sent(zr.at[:, 0, :, pl.ds(0, NB), :], z_s.at[0])
@@ -574,12 +585,17 @@
         place = iota((n, patches), 0).astype(F32)
         member = onehot((place >= end_row - len_row) & (place < end_row))
         spot = iota((patches, NB * PACK), 1).astype(F32)
-        target = route_col * PACK + slot_col * PIECES
-        picks = jnp.concatenate([onehot(spot == target + j) for j in range(PIECES)], axis=0)
-        values = mm(picks, arr2[...]).astype(BF16)
         total = jnp.zeros((patches, w_head.shape[1]), F32)
-        for j in range(PIECES):
-            total = total + mm(values[patches * j : patches * (j + 1), :], w_head[W * j : W * (j + 1), :])
+        for group, count in enumerate((EARLY, LATE)):
+            target = route_col * PACK + slot_col * count
+            picks = jnp.concatenate([onehot(spot == target + j) for j in range(count)], axis=0)
+            exchange_wait(snd2.at[group], arr2.at[group], b_s.at[group], b_r.at[group])
+            values = mm(picks, arr2[group]).astype(BF16)
+            for j in range(count):
+                line = LANES * (EARLY * group + j)
+                total = total + mm(
+                    values[patches * j : patches * (j + 1), :], w_head[line : line + LANES, :]
+                )
         high = total.astype(BF16)
         low = (total - high.astype(F32)).astype(BF16)
         out[...] = (base[...] + mm(member, high) + mm(member, low)).astype(BF16)
@@ -587,10 +603,6 @@
     def own_logits():
         load_wait("head")
         base[...] = mm(states[...], w_head[...])
-
-    def add_residual():
-        load_wait("out")
-        lw[...] = mm(lat[...], w_out[...])
 
     def exch():
         exchange_wait(snd, arr, a_s, a_r)
@@ -612,7 +624,7 @@
         START: start, RELAY: relay, PRODUCT: product, TURN: turn, SUM1: sum1,
         SUM2: sum2, GATHER1: gather1, GATHER2: gather2, GATHER3: gather3,
         JOINED: joined, EXCH: exch, CTXGO: ctx_go, RING: ctx_step, LAT: latents,
-        RES: add_residual, MASK: mask, OWN: own_logits,
+        MASK: mask, OWN: own_logits,
         PROJ: project, HEAD: head, ZF: z_first, ZA: z_add, ZL: z_last,
     }
     load_start()
@@ -628,9 +640,6 @@
     exchange_start(snd, arr, a_s, a_r)
     for name, *where in ORDER:
         stages[name](*where)
-    snd2[...] = packf[...].astype(BF16)
-    exchange_start(snd2, arr2, b_s, b_r)
-    exchange_wait(snd2, arr2, b_s, b_r)
     decode()
     finish()
 
@@ -671,8 +680,8 @@
         buf(PIECES, 2, W, W),
         buf(NB * PACK, W),
         buf(NB * PACK, W),
-        buf(NB * PACK, W),
-        buf(NB * PACK, W),
+        buf(2, NB * PACK, LANES),
+        buf(2, NB * PACK, LANES),
         buf(CTX, E + FLAGS),
         buf(CTX, 2 * W),
         buf(NT, 8, CTX, dtype=F32),
@@ -682,16 +691,15 @@
         buf(CTX, CTX, dtype=F32),
         buf(byte_states.shape[0], w_head.shape[1], dtype=F32),
         buf(4 * NB, 2 * W),
-        buf(CTX, E, dtype=F32),
         buf(PIECES, CTX, W),
         buf(PIECES, 4, 2, 2 * NB, W),
-        buf(NB * PACK, W, dtype=F32),
+        buf(NB * PACK, LANES, dtype=F32),
         dma((2,)), dma((STAGES, 2)), dma, dma((STAGES,)), dma((STAGES,)),
         dma((2,)), dma((2,)), dma, dma, dma((2,)), dma((2, 4, 2)), dma, dma,
         dma((7, 2)),
         dma((STAGES,)), dma((PIECES,)), dma((STAGES,)), dma((STAGES,)), dma((STAGES,)),
         dma((PIECES,)), dma((STAGES,)),
-        dma((2,)), dma((PIECES, 4)), dma, dma,
+        dma((2,)), dma((PIECES, 4)), dma((2,)), dma((2,)),
     ]
     return pl.pallas_call(
         kernel,

time: 93.9 us -> 93.7 us (level)
  no operation moved by 1% of the time
where the time goes in v6:
time: 93.7 us; the launch traced here: 93.6 us
  Pallas kernels  92 us (98%)
  local copies, waits for them, and re-layouts  1.57 us (2%)
    pallas_call x1, Pallas kernels, body(): pl.pallas_call(kernel, out_shape=jax.ShapeDtypeStruct((byte_states.shape[...  92 us

profile of v6, /device:TPU:1, one launch (start us, length us, event | category | flops | bytes accessed | tf_op | source)
XLA Modules:
  0.0 93.6 jit_solution(15333333544101294828)
XLA Ops:
  0.0 92.0 %shard_map.118 = bf16[256,256]{1,0:T(8,128)(2,1)} custom-call(bf16[256,1280]{1,0:T(8,128)(2,1)} %states_far.1, f32[1280]{0:T(1024)} %gain_far.1, s32[1,32]{1,0:T(1,128)} %lengths_far.1, s32[1,32]{1,0:T(1,128)} %bitcast.3, bf16[1280,512]{1,0:T(8,128)(2,1)} %w_in_far.1, f32[32,128]{1,0:T(8,128)} %bitcast.2, bf16[128,512]{1,0:T(8,128)(2,1)} %w_q_far.1, ...), custom_call_target="tpu_custom_call" | custom-call | tf_op jit(solution)/shard_map/pallas_call | solution.py:704
  92.0 1.6 %copy.14 = bf16[256,256]{1,0:T(8,128)(2,1)} copy(bf16[256,256]{1,0:T(8,128)(2,1)} %shard_map.118) | data formatting | bytes 262144
